TPU v7x, 32 devices: a whole 2x2x4 slice. The times are simulated.
32 devices in a mesh: chan: 4 (over z), win: 8 (over y, x, core).
Axes of the slice: x: 2, y: 2, z: 4, core: 2. Of those that a mesh axis runs over, the one named last changes fastest.
Arguments:
- records: bfloat16 [1024, 81920], P('chan', 'win'), may hold values from -50 to 50
- fir_taps: float32 [64], replicated, may hold values from -0.75 to 0.75
- plan: int32 [2, 4], replicated, may hold values from 0 to 3, as said below
Outputs:
- cross: float32 [64, 2, 2, 256, 1024], P('win', None, None, None, 'chan')
Inputs may be any that keep to these rules, and one draw needn't show every extreme that they name: `plan`: in each round block c is paired with block c XOR k for one nonzero key k, the same k for all blocks of the round; the rounds use different keys.
All inputs are finite; a program needn't handle non-finite values.
Results may differ from a plain program's by a relative error of at most 0.02.
Values may be sent and summed in bfloat16 or wider, within the bound.
A program may use at most 128 MiB of HBM per device.

v0:
```python
import math

import jax
import jax.numpy as jnp
from jax import lax
from jax.sharding import PartitionSpec as P

WL = 256
F = 64
TAPS = 64
ROUNDS = 2


def shifted(array, axis, by):
    count = lax.axis_size(axis)
    pairs = [(i, i + by) for i in range(count) if 0 <= i + by < count]
    return lax.ppermute(array, axis, pairs)


def from_partner(block, axis, bit):
    count = lax.axis_size(axis)
    route = []
    for low in range(count):
        high = low | 1 << bit
        if high != low and high < count:
            route += [(low, high), (high, low)]
    return lax.ppermute(block, axis, route)


def fir_matrix(fir_taps):
    inputs_at = jnp.arange(WL + TAPS - 1, dtype=jnp.int32)[:, None]
    outputs_at = jnp.arange(WL, dtype=jnp.int32)[None, :]
    tap_number = outputs_at + (TAPS - 1) - inputs_at
    inside = (tap_number >= 0) & (tap_number < TAPS)
    picked = fir_taps[jnp.clip(tap_number, 0, TAPS - 1)]
    return jnp.where(inside, picked, jnp.zeros_like(picked))


def dft_table():
    sample_at = jnp.arange(WL, dtype=jnp.int32)[:, None]
    column_at = jnp.arange(2 * F, dtype=jnp.int32)[None, :]
    bin_number = column_at // 2 + 1
    phases = (sample_at * bin_number % WL).astype(jnp.float32) * (2.0 * math.pi / WL)
    return jnp.where(column_at % 2 == 0, jnp.cos(phases), -jnp.sin(phases))


def partner_layer(spectra_list):
    layers = []
    for spectra in spectra_list:
        rotated = jnp.stack([-spectra[:, 1], spectra[:, 0]], axis=1)
        layers.append(spectra)
        layers.append(rotated)
    return jnp.concatenate(layers, axis=3)


def cross_term(partner_piece, own_piece, scale):
    product = lax.dot_general(
        partner_piece,
        own_piece,
        (((1, 2), (1, 2)), ((0,), (0,))),
        preferred_element_type=jnp.float32,
    )
    return product * scale


def on_device(records, fir_taps, plan):
    channels, samples_here = records.shape
    window_count = samples_here // WL
    previous_tail = shifted(records[:, samples_here - TAPS + 1 :], "win", 1)
    samples = records.reshape(channels, window_count, WL)
    previous = jnp.concatenate(
        [previous_tail[:, None, :], samples[:, :-1, WL - TAPS + 1 :]], axis=1
    )
    combined_table = jnp.dot(fir_matrix(fir_taps), dft_table(), precision=lax.Precision.HIGHEST)
    stacked = jnp.einsum(
        "cwi,ik->kwc",
        samples.astype(jnp.float32),
        combined_table[TAPS - 1 :],
        precision=lax.Precision.HIGHEST,
    )
    stacked = stacked + jnp.einsum(
        "cwi,ik->kwc",
        previous.astype(jnp.float32),
        combined_table[: TAPS - 1],
        precision=lax.Precision.HIGHEST,
    )
    band_power = jnp.mean(stacked * stacked, axis=0, keepdims=True) + 1e-06
    whitened = (
        (stacked / jnp.sqrt(band_power)).astype(jnp.bfloat16).reshape(F, 2, window_count, channels)
    )
    device_index = lax.axis_index("chan")
    bit_count = lax.axis_size("chan").bit_length() - 1
    win_size = lax.axis_size("win")
    scale = 1.0 / math.sqrt(window_count * win_size)
    chosen = []
    images = [whitened]
    for bit_place in range(bit_count):
        images = images + [from_partner(image, "chan", bit_place) for image in images]
    for round_index in range(ROUNDS):
        offset = jnp.bitwise_xor(plan[round_index, device_index], device_index)
        picked = images[1]
        for key_value in range(2, len(images)):
            picked = jnp.where(offset == key_value, images[key_value], picked)
        chosen.append(picked)
    partner_rows = partner_layer(chosen)
    summed = lax.psum_scatter(
        cross_term(partner_rows, whitened, scale).astype(jnp.bfloat16),
        "win",
        scatter_dimension=0,
        tiled=True,
    ).astype(jnp.float32)
    return summed.reshape(summed.shape[0], ROUNDS, 2, channels, channels)


def solution(mesh):
    placed = (P("chan", "win"), P(), P())
    return jax.shard_map(
        on_device,
        mesh=mesh,
        in_specs=placed,
        out_specs=P("win", None, None, None, "chan"),
        check_vma=False,
    )
```

profile of v0, /device:TPU:0, one launch (start us, length us, event | category | flops | bytes accessed | tf_op | source)
XLA Modules:
  0.0 959.8 jit_solution(17304866313971432415)
XLA Ops:
  6.5 0.0 copy-start
  6.5 0.0 reduce-scatter.2.cloned.1.call-start
  6.5 7.9 copy.11
  14.5 0.8 slice.36
  15.2 2.4 collective-permute-start
  17.6 0.1 compare_select_fusion
  17.8 0.0 copy-done
  17.8 453.5 %gather_fusion = f32[81664]{0:T(1024)S(1)} fusion(f32[64]{0:T(128)S(1)} %copy-done, s32[81920]{0:T(1024)S(1)} %pad_clamp_fusion), kind=kCustom, calls=%fused_computation | custom fusion | bytes 979968 | tf_op jit(solution)/shard_map/gather | solution.py:35
  471.4 0.1 reshape.129
  471.5 1.0 fusion.17
  472.4 5.2 fusion.31
  477.6 2.1 slice.37
  479.7 0.0 collective-permute-done
  479.7 2.9 fusion.12
  482.6 0.6 fusion.13
  483.3 0.0 copy-start.4
  483.3 1.5 copy.22
  484.8 0.0 copy-start.3
  484.8 2.5 collective-permute-start.1
  487.2 2.6 collective-permute-start.3
  489.8 109.7 %collective-permute-done.1 = bf16[64,2,40,256]{3,2,1,0:T(8,128)(2,1)} collective-permute-done((bf16[64,2,40,256]{3,2,1,0:T(8,128)(2,1)S(1)}, bf16[64,2,40,256]{3,2,1,0:T(8,128)(2,1)}, u32[]{:S(2)}, u32[]{:S(2)}) %collective-permute-start.1) | collective-permute-done | bytes 2621472 | tf_op jit(solution)/shard_map/ppermute | solution.py:27
  599.6 1.4 collective-permute-start.2
  601.0 0.0 copy-done.4
  601.0 0.6 constant_dynamic-slice_fusion.1
  602.9 0.0 collective-permute-done.3
  602.9 0.0 copy-done.3
  602.9 113.6 %collective-permute-done.2 = bf16[64,2,40,256]{3,2,1,0:T(8,128)(2,1)} collective-permute-done((bf16[64,2,40,256]{3,2,1,0:T(8,128)(2,1)}, bf16[64,2,40,256]{3,2,1,0:T(8,128)(2,1)}, u32[]{:S(2)}, u32[]{:S(2)}) %collective-permute-start.2) | collective-permute-done | bytes 2621472 | tf_op jit(solution)/shard_map/ppermute | solution.py:27
  716.6 3.7 select_select_fusion.1
  720.3 0.0 copy-start.2
  720.3 2.4 slice_negate_fusion
  722.7 0.6 copy-done.2
  723.3 18.2 %fusion = bf16[64,1024,256]{2,1,0:T(8,128)(2,1)} fusion(bf16[64,2,40,256]{3,2,1,0:T(8,128)(2,1)} %bitcast.36, bf16[64,1,40,256]{3,2,1,0:T(8,128)(2,1)} %get-tuple-element.10, bf16[64,1,40,256]{3,2,1,0:T(8,128)(2,1)} %get-tuple-element.9, bf16[64,2,40,256]{3,2,1,0:T(8,128)(2,1)} %copy-done.2, bf16[64,1,40,256]{3,2,1,0:T(8,128)(2,1)} %get-tuple-element.15, ...), kind=kOutput, calls=%fused_computation.2 | convolution fusion | flops 2780823552 | bytes 46661632 | tf_op jit(solution)/shard_map/dot_general | solution.py:57
  741.6 0.0 reduce-scatter.2.cloned.1.call-update
  741.6 204.8 %reduce-scatter.2.cloned.1.call-done = bf16[8,1024,256]{2,1,0:T(8,128)(2,1)} async-done(((bf16[64,1024,256]{2,1,0:T(8,128)(2,1)}), bf16[8,1024,256]{2,1,0:T(8,128)(2,1)}) %reduce-scatter.2.cloned.1.call-update) | async-done | bytes 4194320 | tf_op jit(solution)/shard_map/reduce_scatter | solution.py:106
  946.3 0.0 copy-start.1
  946.3 6.7 convert.1
  953.0 0.0 copy-done.1
  (6 shorter events, 0.1 us)
Async XLA Ops:
  6.5 11.3 %copy-start = (f32[64]{0:T(128)S(1)}, f32[64]{0:T(128)}, u32[]{:S(2)}) copy-start(f32[64]{0:T(128)} %param.4) | copy-start | bytes 772
  6.5 939.8 %reduce-scatter.2.cloned.1.call-start = ((), (), s32[]{:S(2)}) async-start(), calls=%async_computation.1 | async-start | bytes 37748736 | tf_op jit(solution)/shard_map/reduce_scatter | solution.py:106
  15.2 464.5 %collective-permute-start = (bf16[256,63]{0,1:T(8,128)(2,1)S(1)}, bf16[256,63]{0,1:T(8,128)(2,1)S(1)}, u32[]{:S(2)}, u32[]{:S(2)}) collective-permute-start(bf16[256,63]{0,1:T(8,128)(2,1)S(1)} %slice.36), channel_id=1, source_target_pairs={{0,1},{1,2},{2,3},{3,4},{4,5},{5,6},{6,7},{8,9},{9,10},{10,11},{11... | collective-permute-start | bytes 96776 | tf_op jit(solution)/shard_map/ppermute | solution.py:17
  483.3 117.7 %copy-start.4 = (s32[2,4]{1,0:T(2,128)S(1)}, s32[2,4]{1,0:T(2,128)}, u32[]{:S(2)}) copy-start(s32[2,4]{1,0:T(2,128)} %param.5) | copy-start | bytes 100
  484.8 118.2 %copy-start.3 = (bf16[128,40,256]{2,1,0:T(8,128)(2,1)}, bf16[128,40,256]{2,1,0:T(8,128)(2,1)S(1)}, u32[]{:S(2)}) copy-start(bf16[128,40,256]{2,1,0:T(8,128)(2,1)S(1)} %copy.22) | copy-start | bytes 7864324
  484.8 114.8 %collective-permute-start.1 = (bf16[64,2,40,256]{3,2,1,0:T(8,128)(2,1)S(1)}, bf16[64,2,40,256]{3,2,1,0:T(8,128)(2,1)}, u32[]{:S(2)}, u32[]{:S(2)}) collective-permute-start(bf16[64,2,40,256]{3,2,1,0:T(8,128)(2,1)S(1)} %bitcast.34), channel_id=1, source_target_pairs={{0,8},{8,0},{16,24},{24,16},{1,9},{9,1},{17,25},{25,17},{2,10},{10... | collective-permute-start | bytes 7864328 | tf_op jit(solution)/shard_map/ppermute | solution.py:27
  487.2 115.7 %collective-permute-start.3 = (bf16[64,2,40,256]{3,2,1,0:T(8,128)(2,1)S(1)}, bf16[64,2,40,256]{3,2,1,0:T(8,128)(2,1)}, u32[]{:S(2)}, u32[]{:S(2)}) collective-permute-start(bf16[64,2,40,256]{3,2,1,0:T(8,128)(2,1)S(1)} %bitcast.35), channel_id=1, source_target_pairs={{0,16},{16,0},{8,24},{24,8},{1,17},{17,1},{9,25},{25,9},{2,18},{18... | collective-permute-start | bytes 7864328 | tf_op jit(solution)/shard_map/ppermute | solution.py:27
  599.6 117.0 %collective-permute-start.2 = (bf16[64,2,40,256]{3,2,1,0:T(8,128)(2,1)}, bf16[64,2,40,256]{3,2,1,0:T(8,128)(2,1)}, u32[]{:S(2)}, u32[]{:S(2)}) collective-permute-start(bf16[64,2,40,256]{3,2,1,0:T(8,128)(2,1)} %collective-permute-done.1), channel_id=1, source_target_pairs={{0,16},{16,0},{8,24},{24,8},{1,17},{17,1},{9,25},{25,9},{2,18},{18... | collective-permute-start | bytes 7864328 | tf_op jit(solution)/shard_map/ppermute | solution.py:27
  720.3 3.0 copy-start.2
  946.3 6.7 copy-start.1
Sparse Core Ops, SparseCore 0:
  741.7 204.5 reduce-scatter.1
where the time goes:
time: 960 us
  local copies, waits for them, and re-layouts  467 us (49%)
  waiting for transfers between devices  428 us (45%)
  matrix products  27.3 us (3%)
  between operations  14.9 us (2%)
  other arithmetic  13.6 us (1%)
    gather x2, local copies, waits for them, and re-layouts, fir_matrix(): picked = fir_taps[jnp.clip(tap_number, 0, TAPS - 1)]  454 us
    ppermute x3, waiting for transfers between devices, from_partner(): return lax.ppermute(block, axis, route)  223 us
    reduce_scatter x1, waiting for transfers between devices, on_device(): lax.psum_scatter(cross_term(partner_rows, whitened, scale).astype(jnp.bfl...  205 us
  transfers between devices with their start and end apart: 5, of which 3 were waited for; matrix products, arithmetic and copies ran while one was open for 48% of the time, Pallas kernels for 0%

commit v1 on v0

v1 whole, which is shorter than its diff:
```python
import functools
import math

import jax
import jax.numpy as jnp
from jax import lax
from jax.experimental import pallas as pl
from jax.experimental.pallas import tpu as pltpu
from jax.sharding import PartitionSpec as P

WL = 256
F = 64
TAPS = 64
ROUNDS = 2
MESH = pl.DeviceIdType.MESH


def shifted(array, axis, by):
    count = lax.axis_size(axis)
    pairs = [(i, i + by) for i in range(count) if 0 <= i + by < count]
    return lax.ppermute(array, axis, pairs)


def from_partner(block, axis, bit):
    count = lax.axis_size(axis)
    route = []
    for low in range(count):
        high = low | 1 << bit
        if high != low and high < count:
            route += [(low, high), (high, low)]
    return lax.ppermute(block, axis, route)


def fir_matrix(fir_taps):
    inputs_at = jnp.arange(WL + TAPS - 1, dtype=jnp.int32)[:, None]
    outputs_at = jnp.arange(WL, dtype=jnp.int32)[None, :]
    tap_number = outputs_at + (TAPS - 1) - inputs_at
    inside = (tap_number >= 0) & (tap_number < TAPS)
    picked = fir_taps[jnp.clip(tap_number, 0, TAPS - 1)]
    return jnp.where(inside, picked, jnp.zeros_like(picked))


def dft_table():
    sample_at = jnp.arange(WL, dtype=jnp.int32)[:, None]
    column_at = jnp.arange(2 * F, dtype=jnp.int32)[None, :]
    bin_number = column_at // 2 + 1
    phases = (sample_at * bin_number % WL).astype(jnp.float32) * (2.0 * math.pi / WL)
    return jnp.where(column_at % 2 == 0, jnp.cos(phases), -jnp.sin(phases))


def split_table(fir_taps):
    table = jnp.dot(fir_matrix(fir_taps), dft_table(), precision=lax.Precision.HIGHEST)
    high = table.astype(jnp.bfloat16)
    low = (table - high.astype(jnp.float32)).astype(jnp.bfloat16)
    return jnp.concatenate([high, low], axis=1)


def whiten(records, fir_taps):
    channels, samples_here = records.shape
    window_count = samples_here // WL
    previous_tail = shifted(records[:, samples_here - TAPS + 1 :], "win", 1)
    samples = records.reshape(channels, window_count, WL)
    previous = jnp.concatenate(
        [previous_tail[:, None, :], samples[:, :-1, WL - TAPS + 1 :]], axis=1
    )
    table = split_table(fir_taps)
    both = jnp.einsum(
        "cwi,ik->kwc", samples, table[TAPS - 1 :], preferred_element_type=jnp.float32
    )
    both = both + jnp.einsum(
        "cwi,ik->kwc", previous, table[: TAPS - 1], preferred_element_type=jnp.float32
    )
    stacked = both[: 2 * F] + both[2 * F :]
    band_power = jnp.mean(stacked * stacked, axis=0, keepdims=True) + 1e-06
    return (stacked / jnp.sqrt(band_power)).astype(jnp.bfloat16)


def exchange_kernel(owners, bins, rows, flags, x, gathered, own, recv, stage,
                    a2a_send, a2a_recv, z_send, z_recv, flush_sem):
    chan = lax.axis_index("chan")
    me = lax.axis_index("win")
    is_mid = jnp.logical_and(chan >= 1, chan <= 2)
    is_end = jnp.logical_not(is_mid)
    inner = 3 - chan
    outer = 3 * (chan - 1)
    next_in = 1 + chan // 3

    barrier = pltpu.get_barrier_semaphore()
    for step in range(1, owners):
        pl.semaphore_signal(barrier, inc=1, device_id={"win": lax.rem(me + step, owners)}, device_id_type=MESH)

    @pl.when(is_mid)
    def _():
        pl.semaphore_signal(barrier, inc=1, device_id={"chan": inner}, device_id_type=MESH)
        pl.semaphore_signal(barrier, inc=1, device_id={"chan": outer}, device_id_type=MESH)
        pl.semaphore_wait(barrier, owners + 1)

    @pl.when(is_end)
    def _():
        pl.semaphore_signal(barrier, inc=1, device_id={"chan": next_in}, device_id_type=MESH)
        pl.semaphore_wait(barrier, owners)

    mine = pl.ds(pl.multiple_of(me * rows, rows), rows)

    def start_block(m, carry):
        for step in range(1, owners):
            target = lax.rem(me + step, owners)
            pltpu.make_async_remote_copy(
                src_ref=x.at[target, m], dst_ref=own.at[m, mine],
                send_sem=a2a_send.at[m], recv_sem=a2a_recv.at[m],
                device_id={"win": target}, device_id_type=MESH,
            ).start()
        own[m, mine] = x[me, m]
        return carry

    lax.fori_loop(0, bins, start_block, 0)

    others = pl.ds(0, (owners - 1) * rows)

    def arrived(m):
        pltpu.make_async_copy(own.at[m, others], own.at[m, others], a2a_recv.at[m]).wait()

    def flush(slot, source, m):
        return pltpu.make_async_copy(source.at[m], gathered.at[slot, m], flush_sem.at[slot, m])

    def along(source, slot, m, which, target):
        return pltpu.make_async_remote_copy(
            src_ref=source.at[m], dst_ref=recv.at[slot, m],
            send_sem=z_send.at[which, m], recv_sem=z_recv.at[slot, m],
            device_id={"chan": target}, device_id_type=MESH,
        )

    def got(slot, m):
        pltpu.make_async_copy(recv.at[slot, m], recv.at[slot, m], z_recv.at[slot, m]).wait()

    def when_in(step, lag, body):
        m = step - lag

        @pl.when(jnp.logical_and(m >= 0, m < bins))
        def _():
            body(m)

    @pl.when(is_mid)
    def _():
        has_1 = flags[0] == 1
        has_3 = flags[1] == 1

        def take_own(m):
            arrived(m)
            along(own, 1, m, 0, inner).start()
            flush(0, own, m).start()

        def take_outer(m):
            got(0, m)
            along(recv.at[0], 2, m, 1, inner).start()
            flush(1, recv.at[0], m).start()

        def take_inner(m):
            got(1, m)
            flush(2, recv.at[1], m).start()
            stage[0, m] = jnp.where(has_1, own[m], recv[1, m])
            along(stage.at[0], 0, m, 2, outer).start()

        def take_far(m):
            got(2, m)
            flush(3, recv.at[2], m).start()
            stage[1, m] = jnp.where(has_3, recv[2, m], recv[1, m])
            along(stage.at[1], 1, m, 3, outer).start()

        def step_mid(step, carry):
            when_in(step, 0, take_own)
            when_in(step, 1, take_outer)
            when_in(step, 1, take_inner)
            when_in(step, 2, take_far)
            return carry

        lax.fori_loop(0, bins + 2, step_mid, 0)

        def finish(m, carry):
            along(own, 1, m, 0, inner).wait_send()
            along(recv.at[0], 2, m, 1, inner).wait_send()
            along(stage.at[0], 0, m, 2, outer).wait_send()
            along(stage.at[1], 1, m, 3, outer).wait_send()
            flush(1, recv.at[0], m).wait()
            flush(2, recv.at[1], m).wait()
            flush(3, recv.at[2], m).wait()
            return carry

        lax.fori_loop(0, bins, finish, 0)

    @pl.when(is_end)
    def _():
        def take_own(m):
            arrived(m)
            along(own, 0, m, 0, next_in).start()
            flush(0, own, m).start()

        def take_first(m):
            got(0, m)
            flush(1, recv.at[0], m).start()

        def take_second(m):
            got(1, m)
            flush(2, recv.at[1], m).start()

        def step_end(step, carry):
            when_in(step, 0, take_own)
            when_in(step, 2, take_first)
            when_in(step, 2, take_second)
            return carry

        lax.fori_loop(0, bins + 2, step_end, 0)

        def finish(m, carry):
            along(own, 0, m, 0, next_in).wait_send()
            flush(1, recv.at[0], m).wait()
            flush(2, recv.at[1], m).wait()
            return carry

        lax.fori_loop(0, bins, finish, 0)

    def finish_all(m, carry):
        flush(0, own, m).wait()
        pltpu.make_async_copy(own.at[m, others], own.at[m, others], a2a_send.at[m]).wait()
        return carry

    lax.fori_loop(0, bins, finish_all, 0)


def exchange(x, flags):
    owners, bins, rows, channels = x.shape
    depth = owners * rows
    block = (bins, depth, channels)
    return pl.pallas_call(
        functools.partial(exchange_kernel, owners, bins, rows),
        out_shape=jax.ShapeDtypeStruct((4,) + block, x.dtype),
        in_specs=[pl.BlockSpec(memory_space=pltpu.SMEM), pl.BlockSpec(memory_space=pltpu.VMEM)],
        out_specs=pl.BlockSpec(memory_space=pl.ANY),
        scratch_shapes=[
            pltpu.VMEM(block, x.dtype),
            pltpu.VMEM((3,) + block, x.dtype),
            pltpu.VMEM((2,) + block, x.dtype),
            pltpu.SemaphoreType.DMA((bins,)),
            pltpu.SemaphoreType.DMA((bins,)),
            pltpu.SemaphoreType.DMA((4, bins)),
            pltpu.SemaphoreType.DMA((3, bins)),
            pltpu.SemaphoreType.DMA((4, bins)),
        ],
        compiler_params=pltpu.CompilerParams(
            collective_id=0, has_side_effects=True, vmem_limit_bytes=40 * 1024 * 1024
        ),
        name="exchange",
    )(flags, x)


def cross_kernel(scale, groups, rows, slots, own, first, second, out):
    half = rows // 2
    depth, channels = own.shape
    held = own[...].astype(jnp.float32).reshape(groups, rows, channels)
    turned = jnp.concatenate([held[:, half:], -held[:, :half]], axis=1)
    turned = turned.astype(jnp.bfloat16).reshape(depth, channels)
    for index, partner in enumerate((first, second)):
        for part, right in enumerate((own[...], turned)):
            product = lax.dot_general(
                partner[...], right, (((0,), (0,)), ((), ())), preferred_element_type=jnp.float32
            )
            out[index, part] = product * scale


def cross_terms(gathered, slots, groups, scale):
    _, bins, depth, channels = gathered.shape
    taken = lambda which: pl.BlockSpec(
        (None, None, depth, channels), lambda m, s: (s[which], m, 0, 0)
    )
    return pl.pallas_call(
        functools.partial(cross_kernel, scale, groups, depth // groups),
        out_shape=jax.ShapeDtypeStruct((bins, ROUNDS, 2, channels, channels), jnp.float32),
        grid_spec=pltpu.PrefetchScalarGridSpec(
            num_scalar_prefetch=1,
            grid=(bins,),
            in_specs=[
                pl.BlockSpec((None, None, depth, channels), lambda m, s: (0, m, 0, 0)),
                taken(0),
                taken(1),
            ],
            out_specs=pl.BlockSpec(
                (None, ROUNDS, 2, channels, channels), lambda m, s: (m, 0, 0, 0, 0)
            ),
        ),
        compiler_params=pltpu.CompilerParams(
            dimension_semantics=("arbitrary",), vmem_limit_bytes=40 * 1024 * 1024
        ),
        name="cross",
    )(slots, gathered, gathered, gathered)


def gather_images(x):
    owners, bins, rows, channels = x.shape
    swapped = lax.all_to_all(x, "win", 0, 0, tiled=True)
    images = [swapped.transpose(1, 0, 2, 3).reshape(bins, owners * rows, channels)]
    for bit_place in range(lax.axis_size("chan").bit_length() - 1):
        images = images + [from_partner(image, "chan", bit_place) for image in images]
    return jnp.stack(images)


def on_device(records, fir_taps, plan):
    channels, samples_here = records.shape
    window_count = samples_here // WL
    owners = lax.axis_size("win")
    chan = lax.axis_index("chan")
    scale = 1.0 / math.sqrt(window_count * owners)
    whitened = whiten(records, fir_taps)
    x = whitened.reshape(owners, F // owners, 2 * window_count, channels)
    keys = jnp.bitwise_xor(plan[:, chan], chan)
    if lax.axis_size("chan") == 4:
        has_1 = jnp.any(keys == 1)
        has_3 = jnp.any(keys == 3)
        flags = jnp.stack([has_1, has_3]).astype(jnp.int32)
        gathered = exchange(x, flags)
        at_mid = jnp.where(keys == 1, 1, jnp.where(keys == 3, 2, 3))
        at_end = jnp.where(keys == 1, 1, jnp.where(keys == 3, 2, jnp.where(has_1, 2, 1)))
        slots = jnp.where((chan == 1) | (chan == 2), at_mid, at_end)
    else:
        gathered = gather_images(x)
        slots = keys
    return cross_terms(gathered, slots.astype(jnp.int32), owners, scale)


def solution(mesh):
    placed = (P("chan", "win"), P(), P())
    return jax.shard_map(
        on_device,
        mesh=mesh,
        in_specs=placed,
        out_specs=P("win", None, None, None, "chan"),
        check_vma=False,
    )
```

time: 960 us -> 633 us (0.66)
  waiting for transfers between devices: 428 us -> 0.01 us
  Pallas kernels: 0 us -> 144 us
  between operations: 14.9 us -> 0.72 us
  matrix products: 27.3 us -> 14.6 us
    ppermute x3 -> x0, waiting for transfers between devices: 223 us -> none  [from_partner(): return lax.ppermute(block, axis, route)]
    reduce_scatter x1 -> x0, waiting for transfers between devices: 205 us -> none  [on_device(): lax.psum_scatter(cross_term(partner_rows, whitened, scale).astype(jnp.bfl...]
    pallas_call x0 -> x2, Pallas kernels: none -> 144 us  [the longest x1 137 us: exchange(): pl.pallas_call(functools.partial(exchange_kernel, owners, bins, rows), ou...]
    dot_general x4 -> x3, matrix products: 27.3 us -> 14.6 us  [the longest x1 8.04 us: whiten(): jnp.einsum('cwi,ik->kwc', samples, table[TAPS - 1:], preferred_element_ty...]
  transfers between devices with their start and end apart: 5 -> 1, of which waited for: 3 -> 0; matrix products, arithmetic and copies ran while one was open for 48% -> 74% of each run, Pallas kernels for 0% -> 0%
where the time goes in v1:
time: 633 us
  local copies, waits for them, and re-layouts  466 us (74%)
  Pallas kernels  144 us (23%)
  matrix products  14.6 us (2%)
    gather x2, local copies, waits for them, and re-layouts, fir_matrix(): picked = fir_taps[jnp.clip(tap_number, 0, TAPS - 1)]  454 us
    pallas_call x1, Pallas kernels, exchange(): pl.pallas_call(functools.partial(exchange_kernel, owners, bins, rows), ou...  137 us
  transfers between devices with their start and end apart: 1, of which 0 were waited for; matrix products, arithmetic and copies ran while one was open for 74% of the time, Pallas kernels for 0%

profile of v1, /device:TPU:0, one launch (start us, length us, event | category | flops | bytes accessed | tf_op | source)
XLA Modules:
  0.0 632.6 jit_solution(13068746367107124205)
XLA Ops:
  0.0 0.0 copy-start
  0.0 7.9 %copy.9 = bf16[256,10240]{0,1:T(8,128)(2,1)} copy(bf16[256,10240]{1,0:T(8,128)(2,1)} %param.3) | data formatting | bytes 10485760 | tf_op args[0]
  7.9 0.8 slice.28
  8.7 2.4 collective-permute-start
  11.1 0.1 compare_select_fusion
  11.3 0.0 copy-done
  11.3 0.0 copy-start.1
  11.3 453.5 %gather_fusion = f32[81664]{0:T(1024)S(1)} fusion(f32[64]{0:T(128)S(1)} %copy-done, s32[81920]{0:T(1024)S(1)} %pad_clamp_fusion), kind=kCustom, calls=%fused_computation | custom fusion | bytes 979968 | tf_op jit(solution)/shard_map/gather | solution.py:39
  464.8 0.1 reshape.137
  464.9 0.0 copy-done.1
  464.9 0.8 fusion.44
  465.7 1.0 subtract_convert_fusion
  466.7 8.0 %fusion.16 = f32[256,256,40]{1,0,2:T(8,128)} fusion(bf16[256,40,256]{0,2,1:T(8,128)(2,1)} %bitcast.17, bf16[319,128]{1,0:T(8,128)(2,1)S(1)} %get-tuple-element.8, bf16[319,128]{1,0:T(8,128)(2,1)S(1)} %get-tuple-element.7), kind=kOutput, calls=%fused_computation.28 | convolution fusion | flops 1342439424 | bytes 15891968 | tf_op jit(solution)/shard_map/cwi,ik->kwc/dot_general | solution.py:67
  474.7 1.3 add_convert_fusion.flags
  476.6 2.1 slice.29
  478.7 0.2 select_reduce_fusion.slots
  478.8 0.0 collective-permute-done
  478.9 5.5 add_bitcast_fusion
  484.4 1.2 multiply_reduce_fusion
  485.7 1.3 divide_convert_fusion
  486.9 1.5 copy.13
  488.4 136.5 %exchange.1.own.first.second = bf16[4,8,640,256]{3,2,1,0:T(8,128)(2,1)S(1)} custom-call(s32[2]{0:T(128)S(1)} %add_convert_fusion.flags, bf16[8,8,80,256]{3,2,1,0:T(8,128)(2,1)S(1)} %bitcast.16), custom_call_target="tpu_custom_call" | custom-call | tf_op jit(solution)/shard_map/exchange/pallas_call | solution.py:234
  625.0 7.6 %cross.1 = f32[8,2,2,256,256]{4,3,2,1,0:T(8,128)} custom-call(s32[2]{0:T(128)S(1)} %select_reduce_fusion.slots, bf16[4,8,640,256]{3,2,1,0:T(8,128)(2,1)S(1)} %exchange.1.own.first.second, bf16[4,8,640,256]{3,2,1,0:T(8,128)(2,1)S(1)} %exchange.1.own.first.second, bf16[4,8,640,256]{3,2,1,0:T(8,128)(2,1)S(1)} %exchange.1.own.first.second), custom_call_target="tpu_custom_call" | custom-call | tf_op jit(solution)/shard_map/cross/pallas_call | solution.py:275
  (6 shorter events, 0.1 us)
Async XLA Ops:
  0.0 11.3 %copy-start = (f32[64]{0:T(128)S(1)}, f32[64]{0:T(128)}, u32[]{:S(2)}) copy-start(f32[64]{0:T(128)} %param.4) | copy-start | bytes 772
  8.7 470.2 %collective-permute-start = (bf16[256,63]{0,1:T(8,128)(2,1)S(1)}, bf16[256,63]{0,1:T(8,128)(2,1)S(1)}, u32[]{:S(2)}, u32[]{:S(2)}) collective-permute-start(bf16[256,63]{0,1:T(8,128)(2,1)S(1)} %slice.28), channel_id=1, source_target_pairs={{0,1},{1,2},{2,3},{3,4},{4,5},{5,6},{6,7},{8,9},{9,10},{10,11},{11... | collective-permute-start | bytes 96776 | tf_op jit(solution)/shard_map/ppermute | solution.py:21
  11.3 453.6 %copy-start.1 = (s32[2,4]{1,0:T(2,128)S(1)}, s32[2,4]{1,0:T(2,128)}, u32[]{:S(2)}) copy-start(s32[2,4]{1,0:T(2,128)} %param.5) | copy-start | bytes 100

commit v2 on v1

--- a/solution.py
+++ b/solution.py
@@ -3,6 +3,7 @@
 
 import jax
 import jax.numpy as jnp
+import numpy as np
 from jax import lax
 from jax.experimental import pallas as pl
 from jax.experimental.pallas import tpu as pltpu
@@ -12,6 +13,8 @@
 F = 64
 TAPS = 64
 ROUNDS = 2
+LEFT = 128
+LEAD = 3
 MESH = pl.DeviceIdType.MESH
 
 
@@ -75,8 +78,20 @@
     return (stacked / jnp.sqrt(band_power)).astype(jnp.bfloat16)
 
 
-def exchange_kernel(owners, bins, rows, flags, x, gathered, own, recv, stage,
-                    a2a_send, a2a_recv, z_send, z_recv, flush_sem):
+def dft_rows(owners):
+    bins = F // owners
+    place = np.arange(bins)[:, None, None]
+    owner = np.arange(owners)[None, :, None]
+    part = np.arange(2)[None, None, :]
+    number = np.broadcast_to(owner * bins + place + 1, (bins, owners, 2)).reshape(-1, 1)
+    part = np.broadcast_to(part, (bins, owners, 2)).reshape(-1, 1)
+    phases = (np.arange(WL)[None, :] * number % WL) * (2.0 * np.pi / WL)
+    return np.where(part == 0, np.cos(phases), -np.sin(phases)).astype(np.float32)
+
+
+def exchange_kernel(owners, bins, windows, plan, records, taps, dft, gathered,
+                    table, halo, spectra, x, own, recv, stage,
+                    halo_send, halo_recv, a2a_send, a2a_recv, z_send, z_recv, flush_sem):
     chan = lax.axis_index("chan")
     me = lax.axis_index("win")
     is_mid = jnp.logical_and(chan >= 1, chan <= 2)
@@ -84,6 +99,9 @@
     inner = 3 - chan
     outer = 3 * (chan - 1)
     next_in = 1 + chan // 3
+    rows = 2 * windows
+    kept = 2 * F
+    lanes = spectra.shape[0]
 
     barrier = pltpu.get_barrier_semaphore()
     for step in range(1, owners):
@@ -93,27 +111,82 @@
     def _():
         pl.semaphore_signal(barrier, inc=1, device_id={"chan": inner}, device_id_type=MESH)
         pl.semaphore_signal(barrier, inc=1, device_id={"chan": outer}, device_id_type=MESH)
-        pl.semaphore_wait(barrier, owners + 1)
 
     @pl.when(is_end)
     def _():
         pl.semaphore_signal(barrier, inc=1, device_id={"chan": next_in}, device_id_type=MESH)
-        pl.semaphore_wait(barrier, owners)
+
+    spread = jnp.broadcast_to(taps[...], (LEFT + WL, taps.shape[1]))
+    shifted_taps = pltpu.roll(spread, 0, 1, stride=1, stride_axis=0)[:, LEFT : LEFT + WL]
+    combined = lax.dot_general(
+        dft[...], shifted_taps, (((1,), (1,)), ((), ())),
+        precision=lax.Precision.HIGHEST, preferred_element_type=jnp.float32,
+    )
+    high = combined.astype(jnp.bfloat16)
+    table[:kept] = high
+    table[kept:] = (combined - high.astype(jnp.float32)).astype(jnp.bfloat16)
+
+    pl.semaphore_wait(barrier, jnp.where(is_mid, owners + 1, owners))
+
+    def tail_copy():
+        return pltpu.make_async_remote_copy(
+            src_ref=records.at[:, pl.ds(windows * WL - LEFT, LEFT)], dst_ref=halo,
+            send_sem=halo_send, recv_sem=halo_recv,
+            device_id={"win": lax.rem(me + 1, owners)}, device_id_type=MESH,
+        )
+
+    @pl.when(me < owners - 1)
+    def _():
+        tail_copy().start()
+
+    def whiten_window(w, segment):
+        both = lax.dot_general(
+            table[...], segment, (((1,), (1,)), ((), ())), preferred_element_type=jnp.float32
+        )
+        stacked = both[:kept] + both[kept:]
+        power = jnp.mean(stacked * stacked, axis=0, keepdims=True) + 1e-06
+        whitened = stacked * (1.0 / jnp.sqrt(power))
+        for lane in range(lanes):
+            spectra[lane, pl.ds(pl.multiple_of(w * kept, kept), kept)] = whitened[
+                :, lane * 128 : lane * 128 + 128
+            ]
+
+    def whiten_step(w, carry):
+        start = pl.multiple_of(w * WL - LEFT, LEFT)
+        whiten_window(w, records[:, pl.ds(start, LEFT + WL)])
+        return carry
+
+    lax.fori_loop(1, windows, whiten_step, 0)
+
+    @pl.when(me == 0)
+    def _():
+        halo[...] = jnp.zeros_like(halo)
+
+    @pl.when(me > 0)
+    def _():
+        pltpu.make_async_copy(halo, halo, halo_recv).wait()
+
+    whiten_window(0, jnp.concatenate([halo[...], records[:, :WL]], axis=1))
 
     mine = pl.ds(pl.multiple_of(me * rows, rows), rows)
 
-    def start_block(m, carry):
+    def start_block(m):
+        for owner in range(owners):
+            first = (m * owners + owner) * 2
+            for lane in range(lanes):
+                real = spectra[lane, pl.ds(first, windows, stride=kept)]
+                imag = spectra[lane, pl.ds(first + 1, windows, stride=kept)]
+                x[m, owner, :, lane * 128 : lane * 128 + 128] = jnp.concatenate(
+                    [real, imag], axis=0
+                ).astype(jnp.bfloat16)
         for step in range(1, owners):
             target = lax.rem(me + step, owners)
             pltpu.make_async_remote_copy(
-                src_ref=x.at[target, m], dst_ref=own.at[m, mine],
+                src_ref=x.at[m, target], dst_ref=own.at[m, mine],
                 send_sem=a2a_send.at[m], recv_sem=a2a_recv.at[m],
                 device_id={"win": target}, device_id_type=MESH,
             ).start()
-        own[m, mine] = x[me, m]
-        return carry
-
-    lax.fori_loop(0, bins, start_block, 0)
+        own[m, mine] = x[m, me]
 
     others = pl.ds(0, (owners - 1) * rows)
 
@@ -142,8 +215,8 @@
 
     @pl.when(is_mid)
     def _():
-        has_1 = flags[0] == 1
-        has_3 = flags[1] == 1
+        has_1 = jnp.logical_or(plan[0, 0] == 1, plan[1, 0] == 1)
+        has_3 = jnp.logical_or(plan[0, 0] == 3, plan[1, 0] == 3)
 
         def take_own(m):
             arrived(m)
@@ -168,13 +241,14 @@
             along(stage.at[1], 1, m, 3, outer).start()
 
         def step_mid(step, carry):
-            when_in(step, 0, take_own)
-            when_in(step, 1, take_outer)
-            when_in(step, 1, take_inner)
-            when_in(step, 2, take_far)
+            when_in(step, 0, start_block)
+            when_in(step, LEAD, take_own)
+            when_in(step, LEAD + 1, take_outer)
+            when_in(step, LEAD + 1, take_inner)
+            when_in(step, LEAD + 2, take_far)
             return carry
 
-        lax.fori_loop(0, bins + 2, step_mid, 0)
+        lax.fori_loop(0, bins + LEAD + 2, step_mid, 0)
 
         def finish(m, carry):
             along(own, 1, m, 0, inner).wait_send()
@@ -204,12 +278,13 @@
             flush(2, recv.at[1], m).start()
 
         def step_end(step, carry):
-            when_in(step, 0, take_own)
-            when_in(step, 2, take_first)
-            when_in(step, 2, take_second)
+            when_in(step, 0, start_block)
+            when_in(step, LEAD, take_own)
+            when_in(step, LEAD + 2, take_first)
+            when_in(step, LEAD + 2, take_second)
             return carry
 
-        lax.fori_loop(0, bins + 2, step_end, 0)
+        lax.fori_loop(0, bins + LEAD + 2, step_end, 0)
 
         def finish(m, carry):
             along(own, 0, m, 0, next_in).wait_send()
@@ -226,20 +301,33 @@
 
     lax.fori_loop(0, bins, finish_all, 0)
 
-
-def exchange(x, flags):
-    owners, bins, rows, channels = x.shape
-    depth = owners * rows
-    block = (bins, depth, channels)
+    @pl.when(me < owners - 1)
+    def _():
+        tail_copy().wait_send()
+
+
+def exchange(records, fir_taps, plan):
+    channels, samples_here = records.shape
+    owners = lax.axis_size("win")
+    bins, windows = F // owners, samples_here // WL
+    block = (bins, owners * 2 * windows, channels)
+    taps = jnp.pad(fir_taps[None, :], ((0, 0), (0, LEFT + WL + LEFT - TAPS)))
+    in_vmem = pl.BlockSpec(memory_space=pltpu.VMEM)
     return pl.pallas_call(
-        functools.partial(exchange_kernel, owners, bins, rows),
-        out_shape=jax.ShapeDtypeStruct((4,) + block, x.dtype),
-        in_specs=[pl.BlockSpec(memory_space=pltpu.SMEM), pl.BlockSpec(memory_space=pltpu.VMEM)],
+        functools.partial(exchange_kernel, owners, bins, windows),
+        out_shape=jax.ShapeDtypeStruct((4,) + block, jnp.bfloat16),
+        in_specs=[pl.BlockSpec(memory_space=pltpu.SMEM), in_vmem, in_vmem, in_vmem],
         out_specs=pl.BlockSpec(memory_space=pl.ANY),
         scratch_shapes=[
-            pltpu.VMEM(block, x.dtype),
-            pltpu.VMEM((3,) + block, x.dtype),
-            pltpu.VMEM((2,) + block, x.dtype),
+            pltpu.VMEM((4 * F, LEFT + WL), jnp.bfloat16),
+            pltpu.VMEM((channels, LEFT), jnp.bfloat16),
+            pltpu.VMEM((channels // 128, windows * 2 * F, 128), jnp.float32),
+            pltpu.VMEM((bins, owners, 2 * windows, channels), jnp.bfloat16),
+            pltpu.VMEM(block, jnp.bfloat16),
+            pltpu.VMEM((3,) + block, jnp.bfloat16),
+            pltpu.VMEM((2,) + block, jnp.bfloat16),
+            pltpu.SemaphoreType.DMA,
+            pltpu.SemaphoreType.DMA,
             pltpu.SemaphoreType.DMA((bins,)),
             pltpu.SemaphoreType.DMA((bins,)),
             pltpu.SemaphoreType.DMA((4, bins)),
@@ -247,10 +335,10 @@
             pltpu.SemaphoreType.DMA((4, bins)),
         ],
         compiler_params=pltpu.CompilerParams(
-            collective_id=0, has_side_effects=True, vmem_limit_bytes=40 * 1024 * 1024
+            collective_id=0, has_side_effects=True, vmem_limit_bytes=52 * 1024 * 1024
         ),
         name="exchange",
-    )(flags, x)
+    )(plan, records, taps, jnp.asarray(dft_rows(owners)))
 
 
 def cross_kernel(scale, groups, rows, slots, own, first, second, out):
@@ -309,19 +397,18 @@
     owners = lax.axis_size("win")
     chan = lax.axis_index("chan")
     scale = 1.0 / math.sqrt(window_count * owners)
-    whitened = whiten(records, fir_taps)
-    x = whitened.reshape(owners, F // owners, 2 * window_count, channels)
     keys = jnp.bitwise_xor(plan[:, chan], chan)
     if lax.axis_size("chan") == 4:
         has_1 = jnp.any(keys == 1)
-        has_3 = jnp.any(keys == 3)
-        flags = jnp.stack([has_1, has_3]).astype(jnp.int32)
-        gathered = exchange(x, flags)
+        gathered = exchange(records, fir_taps, plan)
         at_mid = jnp.where(keys == 1, 1, jnp.where(keys == 3, 2, 3))
         at_end = jnp.where(keys == 1, 1, jnp.where(keys == 3, 2, jnp.where(has_1, 2, 1)))
         slots = jnp.where((chan == 1) | (chan == 2), at_mid, at_end)
     else:
-        gathered = gather_images(x)
+        whitened = whiten(records, fir_taps)
+        gathered = gather_images(
+            whitened.reshape(owners, F // owners, 2 * window_count, channels)
+        )
         slots = keys
     return cross_terms(gathered, slots.astype(jnp.int32), owners, scale)
 

time: 633 us -> 166 us (0.26)
  local copies, waits for them, and re-layouts: 466 us -> 6.22 us
  matrix products: 14.6 us -> 0 us
  Pallas kernels: 144 us -> 157 us
    gather x2 -> x0, local copies, waits for them, and re-layouts: 454 us -> none  [fir_matrix(): picked = fir_taps[jnp.clip(tap_number, 0, TAPS - 1)]]
    dot_general x3 -> x0, matrix products: 14.6 us -> none  [the longest x1 8.04 us: whiten(): jnp.einsum('cwi,ik->kwc', samples, table[TAPS - 1:], preferred_element_ty...]
    pallas_call x1, Pallas kernels: 137 us -> 149 us  [exchange(): pl.pallas_call(functools.partial(exchange_kernel, owners, bins, windows),...]
  transfers between devices with their start and end apart: 1 -> 0, of which waited for: 0 -> 0; matrix products, arithmetic and copies ran while one was open for 74% -> 0% of each run, Pallas kernels for 0% -> 0%
where the time goes in v2:
time: 166 us
  Pallas kernels  157 us (95%)
  local copies, waits for them, and re-layouts  6.22 us (4%)
  other arithmetic  2.26 us (1%)
    pallas_call x1, Pallas kernels, exchange(): pl.pallas_call(functools.partial(exchange_kernel, owners, bins, windows),...  149 us
    pallas_call x1, Pallas kernels, cross_terms(): pl.pallas_call(functools.partial(cross_kernel, scale, groups, depth // gr...  7.6 us
    unnamed x6, local copies, waits for them, and re-layouts  5.55 us

profile of v2, /device:TPU:0, one launch (start us, length us, event | category | flops | bytes accessed | tf_op | source)
XLA Modules:
  0.0 165.7 jit_solution(12290305471725985652)
XLA Ops:
  0.0 1.4 fusion
  2.0 0.9 select_reduce_fusion.slots
  2.9 0.7 pad.4.taps
  3.6 0.0 copy-start.1
  3.6 0.9 copy-done.1
  4.5 0.0 copy-start.2
  4.5 0.7 copy-done.2
  5.2 149.0 %exchange.1.own.first.second = bf16[4,8,640,256]{3,2,1,0:T(8,128)(2,1)} custom-call(s32[2,4]{1,0:T(2,128)S(1)} %copy-done.2, bf16[256,10240]{1,0:T(8,128)(2,1)} %records.1, f32[1,512]{1,0:T(1,128)S(1)} %pad.4.taps, f32[128,256]{1,0:T(8,128)S(1)} %copy-done.1), custom_call_target="tpu_custom_call" | custom-call | tf_op jit(solution)/shard_map/exchange/pallas_call | solution.py:316
  154.2 0.0 copy-start
  154.2 4.0 %copy-done = bf16[4,8,640,256]{3,2,1,0:T(8,128)(2,1)S(1)} copy-done((bf16[4,8,640,256]{3,2,1,0:T(8,128)(2,1)S(1)}, bf16[4,8,640,256]{3,2,1,0:T(8,128)(2,1)}, u32[]{:S(2)}) %copy-start) | copy-done | bytes 10485784
  158.1 7.6 %cross.1 = f32[8,2,2,256,256]{4,3,2,1,0:T(8,128)} custom-call(s32[2]{0:T(128)S(1)} %select_reduce_fusion.slots, bf16[4,8,640,256]{3,2,1,0:T(8,128)(2,1)S(1)} %copy-done, bf16[4,8,640,256]{3,2,1,0:T(8,128)(2,1)S(1)} %copy-done, bf16[4,8,640,256]{3,2,1,0:T(8,128)(2,1)S(1)} %copy-done), custom_call_target="tpu_custom_call" | custom-call | tf_op jit(solution)/shard_map/cross/pallas_call | solution.py:363
Async XLA Ops:
  3.6 0.9 copy-start.1
  4.5 0.7 copy-start.2
  154.2 4.0 %copy-start = (bf16[4,8,640,256]{3,2,1,0:T(8,128)(2,1)S(1)}, bf16[4,8,640,256]{3,2,1,0:T(8,128)(2,1)}, u32[]{:S(2)}) copy-start(bf16[4,8,640,256]{3,2,1,0:T(8,128)(2,1)} %exchange.1.own.first.second) | copy-start | bytes 31457284

commit v3 on v2

--- a/solution.py
+++ b/solution.py
@@ -14,7 +14,9 @@
 TAPS = 64
 ROUNDS = 2
 LEFT = 128
-LEAD = 3
+GROUP = 8
+PER_CHUNK = 2
+LEAD = 4
 MESH = pl.DeviceIdType.MESH
 
 
@@ -89,9 +91,9 @@
     return np.where(part == 0, np.cos(phases), -np.sin(phases)).astype(np.float32)
 
 
-def exchange_kernel(owners, bins, windows, plan, records, taps, dft, gathered,
-                    table, halo, spectra, x, own, recv, stage,
-                    halo_send, halo_recv, a2a_send, a2a_recv, z_send, z_recv, flush_sem):
+def exchange_kernel(owners, bins, windows, scale, plan, records, taps, dft, out,
+                    rec, table, halo, spectra, x, own, recv, stage, acc, result,
+                    rec_sem, halo_send, halo_recv, a2a_send, a2a_recv, z_send, z_recv, out_sem):
     chan = lax.axis_index("chan")
     me = lax.axis_index("win")
     is_mid = jnp.logical_and(chan >= 1, chan <= 2)
@@ -99,9 +101,20 @@
     inner = 3 - chan
     outer = 3 * (chan - 1)
     next_in = 1 + chan // 3
-    rows = 2 * windows
     kept = 2 * F
     lanes = spectra.shape[0]
+    groups = windows // GROUP
+    pairs = bins // PER_CHUNK
+    chunks = groups * pairs
+    span = GROUP * WL
+    unit = 2 * GROUP
+
+    def load(g):
+        columns = pl.ds(pl.multiple_of(g * span, span), span)
+        return pltpu.make_async_copy(records.at[:, columns], rec.at[:, columns], rec_sem.at[g])
+
+    for g in range(groups):
+        load(g).start()
 
     barrier = pltpu.get_barrier_semaphore()
     for step in range(1, owners):
@@ -139,7 +152,7 @@
     def _():
         tail_copy().start()
 
-    def whiten_window(w, segment):
+    def whiten_window(place, segment):
         both = lax.dot_general(
             table[...], segment, (((1,), (1,)), ((), ())), preferred_element_type=jnp.float32
         )
@@ -147,195 +160,251 @@
         power = jnp.mean(stacked * stacked, axis=0, keepdims=True) + 1e-06
         whitened = stacked * (1.0 / jnp.sqrt(power))
         for lane in range(lanes):
-            spectra[lane, pl.ds(pl.multiple_of(w * kept, kept), kept)] = whitened[
-                :, lane * 128 : lane * 128 + 128
-            ]
-
-    def whiten_step(w, carry):
-        start = pl.multiple_of(w * WL - LEFT, LEFT)
-        whiten_window(w, records[:, pl.ds(start, LEFT + WL)])
-        return carry
-
-    lax.fori_loop(1, windows, whiten_step, 0)
-
-    @pl.when(me == 0)
-    def _():
-        halo[...] = jnp.zeros_like(halo)
-
-    @pl.when(me > 0)
-    def _():
-        pltpu.make_async_copy(halo, halo, halo_recv).wait()
-
-    whiten_window(0, jnp.concatenate([halo[...], records[:, :WL]], axis=1))
-
-    mine = pl.ds(pl.multiple_of(me * rows, rows), rows)
-
-    def start_block(m):
-        for owner in range(owners):
-            first = (m * owners + owner) * 2
-            for lane in range(lanes):
-                real = spectra[lane, pl.ds(first, windows, stride=kept)]
-                imag = spectra[lane, pl.ds(first + 1, windows, stride=kept)]
-                x[m, owner, :, lane * 128 : lane * 128 + 128] = jnp.concatenate(
-                    [real, imag], axis=0
-                ).astype(jnp.bfloat16)
+            spectra[lane, pl.ds(place * kept, kept)] = whitened[:, lane * 128 : lane * 128 + 128]
+
+    def whiten_group(turn):
+        g = lax.rem(turn + 1, groups)
+        base = g * span
+
+        @pl.when(turn == 0)
+        def _():
+            load(0).wait()
+
+        @pl.when(g > 0)
+        def _():
+            load(g).wait()
+            whiten_window(0, rec[:, pl.ds(pl.multiple_of(base - LEFT, LEFT), LEFT + WL)])
+
+        @pl.when(jnp.logical_and(g == 0, me == 0))
+        def _():
+            halo[...] = jnp.zeros_like(halo)
+
+        @pl.when(jnp.logical_and(g == 0, me > 0))
+        def _():
+            pltpu.make_async_copy(halo, halo, halo_recv).wait()
+
+        @pl.when(g == 0)
+        def _():
+            whiten_window(0, jnp.concatenate([halo[...], rec[:, :WL]], axis=1))
+
+        for place in range(1, GROUP):
+            start = pl.multiple_of(base + place * WL - LEFT, LEFT)
+            whiten_window(place, rec[:, pl.ds(start, LEFT + WL)])
+
+    mine = pl.ds(pl.multiple_of(me * unit, unit), unit)
+
+    def start_block(n):
+        pair = lax.rem(n, pairs)
+
+        @pl.when(pair == 0)
+        def _():
+            whiten_group(n // pairs)
+
+        for b in range(PER_CHUNK):
+            for owner in range(owners):
+                first = ((pair * PER_CHUNK + b) * owners + owner) * 2
+                for lane in range(lanes):
+                    real = spectra[lane, pl.ds(first, GROUP, stride=kept)]
+                    imag = spectra[lane, pl.ds(first + 1, GROUP, stride=kept)]
+                    x[n, owner, b, :, lane * 128 : lane * 128 + 128] = jnp.concatenate(
+                        [real, imag], axis=0
+                    ).astype(jnp.bfloat16)
         for step in range(1, owners):
             target = lax.rem(me + step, owners)
             pltpu.make_async_remote_copy(
-                src_ref=x.at[m, target], dst_ref=own.at[m, mine],
-                send_sem=a2a_send.at[m], recv_sem=a2a_recv.at[m],
+                src_ref=x.at[n, target], dst_ref=own.at[n, :, mine],
+                send_sem=a2a_send.at[n], recv_sem=a2a_recv.at[n],
                 device_id={"win": target}, device_id_type=MESH,
             ).start()
-        own[m, mine] = x[m, me]
-
-    others = pl.ds(0, (owners - 1) * rows)
-
-    def arrived(m):
-        pltpu.make_async_copy(own.at[m, others], own.at[m, others], a2a_recv.at[m]).wait()
-
-    def flush(slot, source, m):
-        return pltpu.make_async_copy(source.at[m], gathered.at[slot, m], flush_sem.at[slot, m])
-
-    def along(source, slot, m, which, target):
+        own[n, :, mine] = x[n, me]
+
+    others = pl.ds(0, (owners - 1) * unit)
+
+    def arrived(n):
+        pltpu.make_async_copy(own.at[n, :, others], own.at[n, :, others], a2a_recv.at[n]).wait()
+
+    def along(source, slot, n, which, target):
         return pltpu.make_async_remote_copy(
-            src_ref=source.at[m], dst_ref=recv.at[slot, m],
-            send_sem=z_send.at[which, m], recv_sem=z_recv.at[slot, m],
+            src_ref=source.at[n], dst_ref=recv.at[slot, n],
+            send_sem=z_send.at[which, n], recv_sem=z_recv.at[slot, n],
             device_id={"chan": target}, device_id_type=MESH,
         )
 
-    def got(slot, m):
-        pltpu.make_async_copy(recv.at[slot, m], recv.at[slot, m], z_recv.at[slot, m]).wait()
+    def got(slot, n):
+        pltpu.make_async_copy(recv.at[slot, n], recv.at[slot, n], z_recv.at[slot, n]).wait()
+
+    def flush(pair):
+        place = pl.ds(pair * PER_CHUNK, PER_CHUNK)
+        return pltpu.make_async_copy(result.at[place], out.at[place], out_sem.at[pair])
+
+    def multiply(n, choose):
+        pair = lax.rem(n, pairs)
+        started = n >= pairs
+        for b in range(PER_CHUNK):
+            at = pair * PER_CHUNK + b
+            mine_now = own[n, b]
+            depth, channels = mine_now.shape
+            held = mine_now.astype(jnp.float32).reshape(owners, unit, channels)
+            turned = jnp.concatenate([held[:, GROUP:], -held[:, :GROUP]], axis=1)
+            turned = turned.astype(jnp.bfloat16).reshape(depth, channels)
+            right = jnp.concatenate([mine_now, turned], axis=1)
+            for index in range(ROUNDS):
+                product = lax.dot_general(
+                    choose(index, b), right, (((0,), (0,)), ((), ())),
+                    preferred_element_type=jnp.float32,
+                )
+                acc[at, index] = jnp.where(started, acc[at, index], 0.0) + product
+
+        @pl.when(n >= chunks - pairs)
+        def _():
+            for b in range(PER_CHUNK):
+                at = pair * PER_CHUNK + b
+                for index in range(ROUNDS):
+                    total = (acc[at, index] * scale).astype(result.dtype)
+                    for part in range(2):
+                        result[at, index, part] = total[:, part * channels : (part + 1) * channels]
+            flush(pair).start()
 
     def when_in(step, lag, body):
-        m = step - lag
-
-        @pl.when(jnp.logical_and(m >= 0, m < bins))
-        def _():
-            body(m)
+        n = step - lag
+
+        @pl.when(jnp.logical_and(n >= 0, n < chunks))
+        def _():
+            body(n)
+
+    keys = [plan[index, 0] for index in range(ROUNDS)]
+    has_1 = jnp.logical_or(keys[0] == 1, keys[1] == 1)
+    has_3 = jnp.logical_or(keys[0] == 3, keys[1] == 3)
 
     @pl.when(is_mid)
     def _():
-        has_1 = jnp.logical_or(plan[0, 0] == 1, plan[1, 0] == 1)
-        has_3 = jnp.logical_or(plan[0, 0] == 3, plan[1, 0] == 3)
-
-        def take_own(m):
-            arrived(m)
-            along(own, 1, m, 0, inner).start()
-            flush(0, own, m).start()
-
-        def take_outer(m):
-            got(0, m)
-            along(recv.at[0], 2, m, 1, inner).start()
-            flush(1, recv.at[0], m).start()
-
-        def take_inner(m):
-            got(1, m)
-            flush(2, recv.at[1], m).start()
-            stage[0, m] = jnp.where(has_1, own[m], recv[1, m])
-            along(stage.at[0], 0, m, 2, outer).start()
-
-        def take_far(m):
-            got(2, m)
-            flush(3, recv.at[2], m).start()
-            stage[1, m] = jnp.where(has_3, recv[2, m], recv[1, m])
-            along(stage.at[1], 1, m, 3, outer).start()
+        def take_own(n):
+            arrived(n)
+            along(own, 1, n, 0, inner).start()
+
+        def take_outer(n):
+            got(0, n)
+            along(recv.at[0], 2, n, 1, inner).start()
+
+        def take_inner(n):
+            got(1, n)
+            stage[0, n] = jnp.where(has_1, own[n], recv[1, n])
+            along(stage.at[0], 0, n, 2, outer).start()
+
+        def take_far(n):
+            got(2, n)
+            stage[1, n] = jnp.where(has_3, recv[2, n], recv[1, n])
+            along(stage.at[1], 1, n, 3, outer).start()
+
+            def choose(index, b):
+                key = keys[index]
+                later = jnp.where(key == 3, recv[1, n, b], recv[2, n, b])
+                return jnp.where(key == 1, recv[0, n, b], later)
+
+            multiply(n, choose)
 
         def step_mid(step, carry):
             when_in(step, 0, start_block)
             when_in(step, LEAD, take_own)
             when_in(step, LEAD + 1, take_outer)
-            when_in(step, LEAD + 1, take_inner)
-            when_in(step, LEAD + 2, take_far)
+            when_in(step, LEAD + 2, take_inner)
+            when_in(step, LEAD + 3, take_far)
             return carry
 
-        lax.fori_loop(0, bins + LEAD + 2, step_mid, 0)
-
-        def finish(m, carry):
-            along(own, 1, m, 0, inner).wait_send()
-            along(recv.at[0], 2, m, 1, inner).wait_send()
-            along(stage.at[0], 0, m, 2, outer).wait_send()
-            along(stage.at[1], 1, m, 3, outer).wait_send()
-            flush(1, recv.at[0], m).wait()
-            flush(2, recv.at[1], m).wait()
-            flush(3, recv.at[2], m).wait()
+        lax.fori_loop(0, chunks + LEAD + 3, step_mid, 0)
+
+        def finish(n, carry):
+            along(own, 1, n, 0, inner).wait_send()
+            along(recv.at[0], 2, n, 1, inner).wait_send()
+            along(stage.at[0], 0, n, 2, outer).wait_send()
+            along(stage.at[1], 1, n, 3, outer).wait_send()
             return carry
 
-        lax.fori_loop(0, bins, finish, 0)
+        lax.fori_loop(0, chunks, finish, 0)
 
     @pl.when(is_end)
     def _():
-        def take_own(m):
-            arrived(m)
-            along(own, 0, m, 0, next_in).start()
-            flush(0, own, m).start()
-
-        def take_first(m):
-            got(0, m)
-            flush(1, recv.at[0], m).start()
-
-        def take_second(m):
-            got(1, m)
-            flush(2, recv.at[1], m).start()
+        def take_own(n):
+            arrived(n)
+            along(own, 0, n, 0, next_in).start()
+
+        def take_both(n):
+            got(0, n)
+            got(1, n)
+
+            def choose(index, b):
+                key = keys[index]
+                in_first = jnp.logical_or(
+                    key == 1, jnp.logical_and(key == 2, jnp.logical_not(has_1))
+                )
+                return jnp.where(in_first, recv[0, n, b], recv[1, n, b])
+
+            multiply(n, choose)
 
         def step_end(step, carry):
             when_in(step, 0, start_block)
             when_in(step, LEAD, take_own)
-            when_in(step, LEAD + 2, take_first)
-            when_in(step, LEAD + 2, take_second)
+            when_in(step, LEAD + 5, take_both)
             return carry
 
-        lax.fori_loop(0, bins + LEAD + 2, step_end, 0)
-
-        def finish(m, carry):
-            along(own, 0, m, 0, next_in).wait_send()
-            flush(1, recv.at[0], m).wait()
-            flush(2, recv.at[1], m).wait()
+        lax.fori_loop(0, chunks + LEAD + 5, step_end, 0)
+
+        def finish(n, carry):
+            along(own, 0, n, 0, next_in).wait_send()
             return carry
 
-        lax.fori_loop(0, bins, finish, 0)
-
-    def finish_all(m, carry):
-        flush(0, own, m).wait()
-        pltpu.make_async_copy(own.at[m, others], own.at[m, others], a2a_send.at[m]).wait()
+        lax.fori_loop(0, chunks, finish, 0)
+
+    def finish_all(n, carry):
+        pltpu.make_async_copy(own.at[n, :, others], own.at[n, :, others], a2a_send.at[n]).wait()
         return carry
 
-    lax.fori_loop(0, bins, finish_all, 0)
+    lax.fori_loop(0, chunks, finish_all, 0)
+    for pair in range(pairs):
+        flush(pair).wait()
 
     @pl.when(me < owners - 1)
     def _():
         tail_copy().wait_send()
 
 
-def exchange(records, fir_taps, plan):
+def exchange(records, fir_taps, plan, scale):
     channels, samples_here = records.shape
     owners = lax.axis_size("win")
     bins, windows = F // owners, samples_here // WL
-    block = (bins, owners * 2 * windows, channels)
+    chunks = (windows // GROUP) * (bins // PER_CHUNK)
+    block = (chunks, PER_CHUNK, owners * 2 * GROUP, channels)
     taps = jnp.pad(fir_taps[None, :], ((0, 0), (0, LEFT + WL + LEFT - TAPS)))
     in_vmem = pl.BlockSpec(memory_space=pltpu.VMEM)
+    in_place = pl.BlockSpec(memory_space=pl.ANY)
+    result = (bins, ROUNDS, 2, channels, channels)
     return pl.pallas_call(
-        functools.partial(exchange_kernel, owners, bins, windows),
-        out_shape=jax.ShapeDtypeStruct((4,) + block, jnp.bfloat16),
-        in_specs=[pl.BlockSpec(memory_space=pltpu.SMEM), in_vmem, in_vmem, in_vmem],
-        out_specs=pl.BlockSpec(memory_space=pl.ANY),
+        functools.partial(exchange_kernel, owners, bins, windows, scale),
+        out_shape=jax.ShapeDtypeStruct(result, jnp.bfloat16),
+        in_specs=[pl.BlockSpec(memory_space=pltpu.SMEM), in_place, in_vmem, in_vmem],
+        out_specs=in_place,
         scratch_shapes=[
+            pltpu.VMEM(records.shape, jnp.bfloat16),
             pltpu.VMEM((4 * F, LEFT + WL), jnp.bfloat16),
             pltpu.VMEM((channels, LEFT), jnp.bfloat16),
-            pltpu.VMEM((channels // 128, windows * 2 * F, 128), jnp.float32),
-            pltpu.VMEM((bins, owners, 2 * windows, channels), jnp.bfloat16),
+            pltpu.VMEM((channels // 128, GROUP * 2 * F, 128), jnp.float32),
+            pltpu.VMEM((chunks, owners, PER_CHUNK, 2 * GROUP, channels), jnp.bfloat16),
             pltpu.VMEM(block, jnp.bfloat16),
             pltpu.VMEM((3,) + block, jnp.bfloat16),
             pltpu.VMEM((2,) + block, jnp.bfloat16),
+            pltpu.VMEM((bins, ROUNDS, channels, 2 * channels), jnp.float32),
+            pltpu.VMEM(result, jnp.bfloat16),
+            pltpu.SemaphoreType.DMA((windows // GROUP,)),
             pltpu.SemaphoreType.DMA,
             pltpu.SemaphoreType.DMA,
-            pltpu.SemaphoreType.DMA((bins,)),
-            pltpu.SemaphoreType.DMA((bins,)),
-            pltpu.SemaphoreType.DMA((4, bins)),
-            pltpu.SemaphoreType.DMA((3, bins)),
-            pltpu.SemaphoreType.DMA((4, bins)),
+            pltpu.SemaphoreType.DMA((chunks,)),
+            pltpu.SemaphoreType.DMA((chunks,)),
+            pltpu.SemaphoreType.DMA((4, chunks)),
+            pltpu.SemaphoreType.DMA((3, chunks)),
+            pltpu.SemaphoreType.DMA((bins // PER_CHUNK,)),
         ],
         compiler_params=pltpu.CompilerParams(
-            collective_id=0, has_side_effects=True, vmem_limit_bytes=52 * 1024 * 1024
+            collective_id=0, has_side_effects=True, vmem_limit_bytes=48 * 1024 * 1024
         ),
         name="exchange",
     )(plan, records, taps, jnp.asarray(dft_rows(owners)))
@@ -399,18 +468,12 @@
     scale = 1.0 / math.sqrt(window_count * owners)
     keys = jnp.bitwise_xor(plan[:, chan], chan)
     if lax.axis_size("chan") == 4:
-        has_1 = jnp.any(keys == 1)
-        gathered = exchange(records, fir_taps, plan)
-        at_mid = jnp.where(keys == 1, 1, jnp.where(keys == 3, 2, 3))
-        at_end = jnp.where(keys == 1, 1, jnp.where(keys == 3, 2, jnp.where(has_1, 2, 1)))
-        slots = jnp.where((chan == 1) | (chan == 2), at_mid, at_end)
-    else:
-        whitened = whiten(records, fir_taps)
-        gathered = gather_images(
-            whitened.reshape(owners, F // owners, 2 * window_count, channels)
-        )
-        slots = keys
-    return cross_terms(gathered, slots.astype(jnp.int32), owners, scale)
+        return exchange(records, fir_taps, plan, scale).astype(jnp.float32)
+    whitened = whiten(records, fir_taps)
+    gathered = gather_images(
+        whitened.reshape(owners, F // owners, 2 * window_count, channels)
+    )
+    return cross_terms(gathered, keys.astype(jnp.int32), owners, scale)
 
 
 def solution(mesh):

time: 166 us -> 141 us (0.85)
  Pallas kernels: 157 us -> 134 us
  local copies, waits for them, and re-layouts: 6.22 us -> 2.24 us
  other arithmetic: 2.26 us -> 4.45 us
    pallas_call x2 -> x1, Pallas kernels: 157 us -> 134 us  [exchange(): pl.pallas_call(functools.partial(exchange_kernel, owners, bins, windows,...]
    convert_element_type x0 -> x1, other arithmetic: none -> 4.45 us  [on_device(): return exchange(records, fir_taps, plan, scale).astype(jnp.float32)]
    unnamed x6 -> x4, local copies, waits for them, and re-layouts: 5.55 us -> 1.58 us
where the time goes in v3:
time: 141 us
  Pallas kernels  134 us (95%)
  other arithmetic  4.45 us (3%)
  local copies, waits for them, and re-layouts  2.24 us (2%)
    pallas_call x1, Pallas kernels, exchange(): pl.pallas_call(functools.partial(exchange_kernel, owners, bins, windows,...  134 us
    convert_element_type x1, other arithmetic, on_device(): return exchange(records, fir_taps, plan, scale).astype(jnp.float32)  4.45 us

profile of v3, /device:TPU:0, one launch (start us, length us, event | category | flops | bytes accessed | tf_op | source)
XLA Modules:
  0.0 140.5 jit_solution(14919839428517233710)
XLA Ops:
  0.0 0.7 pad.4.taps
  0.7 0.0 copy-start
  0.7 0.9 copy-done
  1.6 0.0 copy-start.1
  1.6 0.7 copy-done.1
  2.2 133.8 %exchange.1 = bf16[8,2,2,256,256]{4,3,2,1,0:T(8,128)(2,1)S(1)} custom-call(s32[2,4]{1,0:T(2,128)S(1)} %copy-done.1, bf16[256,10240]{1,0:T(8,128)(2,1)} %records.1, f32[1,512]{1,0:T(1,128)S(1)} %pad.4.taps, f32[128,256]{1,0:T(8,128)S(1)} %copy-done), custom_call_target="tpu_custom_call" | custom-call | tf_op jit(solution)/shard_map/exchange/pallas_call | solution.py:381
  136.1 4.5 %convert_element_type.5 = f32[8,2,2,256,256]{4,3,2,1,0:T(8,128)} convert(bf16[8,2,2,256,256]{4,3,2,1,0:T(8,128)(2,1)S(1)} %exchange.1) | non-fusion elementwise | flops 2097152 | bytes 12582912 | tf_op jit(solution)/shard_map/convert_element_type | solution.py:471
Async XLA Ops:
  0.7 0.9 copy-start
  1.6 0.7 copy-start.1

commit v4 on v3

--- a/solution.py
+++ b/solution.py
@@ -15,7 +15,7 @@
 ROUNDS = 2
 LEFT = 128
 GROUP = 8
-PER_CHUNK = 2
+PER_CHUNK = 1
 LEAD = 4
 MESH = pl.DeviceIdType.MESH
 
@@ -91,9 +91,9 @@
     return np.where(part == 0, np.cos(phases), -np.sin(phases)).astype(np.float32)
 
 
-def exchange_kernel(owners, bins, windows, scale, plan, records, taps, dft, out,
-                    rec, table, halo, spectra, x, own, recv, stage, acc, result,
-                    rec_sem, halo_send, halo_recv, a2a_send, a2a_recv, z_send, z_recv, out_sem):
+def exchange_kernel(owners, bins, windows, scale, plan_at, records, taps_at, dft_at, out,
+                    plan, taps, dft, rec, table, halo, spectra, x, own, recv, stage, acc, result,
+                    small_sem, rec_sem, halo_send, halo_recv, a2a_send, a2a_recv, z_send, z_recv, out_sem):
     chan = lax.axis_index("chan")
     me = lax.axis_index("win")
     is_mid = jnp.logical_and(chan >= 1, chan <= 2)
@@ -113,6 +113,12 @@
         columns = pl.ds(pl.multiple_of(g * span, span), span)
         return pltpu.make_async_copy(records.at[:, columns], rec.at[:, columns], rec_sem.at[g])
 
+    small = [
+        pltpu.make_async_copy(source, target, small_sem.at[place])
+        for place, (source, target) in enumerate(((taps_at, taps), (dft_at, dft), (plan_at, plan)))
+    ]
+    for copy in small:
+        copy.start()
     for g in range(groups):
         load(g).start()
 
@@ -129,7 +135,10 @@
     def _():
         pl.semaphore_signal(barrier, inc=1, device_id={"chan": next_in}, device_id_type=MESH)
 
-    spread = jnp.broadcast_to(taps[...], (LEFT + WL, taps.shape[1]))
+    for copy in small:
+        copy.wait()
+    row = jnp.concatenate([taps[...], jnp.zeros((1, LEFT + WL + LEFT - TAPS), jnp.float32)], axis=1)
+    spread = jnp.broadcast_to(row, (LEFT + WL, LEFT + WL + LEFT))
     shifted_taps = pltpu.roll(spread, 0, 1, stride=1, stride_axis=0)[:, LEFT : LEFT + WL]
     combined = lax.dot_general(
         dft[...], shifted_taps, (((1,), (1,)), ((), ())),
@@ -247,22 +256,19 @@
             held = mine_now.astype(jnp.float32).reshape(owners, unit, channels)
             turned = jnp.concatenate([held[:, GROUP:], -held[:, :GROUP]], axis=1)
             turned = turned.astype(jnp.bfloat16).reshape(depth, channels)
-            right = jnp.concatenate([mine_now, turned], axis=1)
             for index in range(ROUNDS):
-                product = lax.dot_general(
-                    choose(index, b), right, (((0,), (0,)), ((), ())),
-                    preferred_element_type=jnp.float32,
-                )
-                acc[at, index] = jnp.where(started, acc[at, index], 0.0) + product
+                partner = choose(index, b)
+                for part, right in enumerate((mine_now, turned)):
+                    product = lax.dot_general(
+                        partner, right, (((0,), (0,)), ((), ())),
+                        preferred_element_type=jnp.float32,
+                    )
+                    total = jnp.where(started, acc[at, index, part], 0.0) + product
+                    acc[at, index, part] = total
+                    result[at, index, part] = (total * scale).astype(result.dtype)
 
         @pl.when(n >= chunks - pairs)
         def _():
-            for b in range(PER_CHUNK):
-                at = pair * PER_CHUNK + b
-                for index in range(ROUNDS):
-                    total = (acc[at, index] * scale).astype(result.dtype)
-                    for part in range(2):
-                        result[at, index, part] = total[:, part * channels : (part + 1) * channels]
             flush(pair).start()
 
     def when_in(step, lag, body):
@@ -296,6 +302,7 @@
             stage[1, n] = jnp.where(has_3, recv[2, n], recv[1, n])
             along(stage.at[1], 1, n, 3, outer).start()
 
+        def multiply_mid(n):
             def choose(index, b):
                 key = keys[index]
                 later = jnp.where(key == 3, recv[1, n, b], recv[2, n, b])
@@ -304,14 +311,15 @@
             multiply(n, choose)
 
         def step_mid(step, carry):
-            when_in(step, 0, start_block)
             when_in(step, LEAD, take_own)
             when_in(step, LEAD + 1, take_outer)
             when_in(step, LEAD + 2, take_inner)
-            when_in(step, LEAD + 3, take_far)
+            when_in(step, LEAD + 4, take_far)
+            when_in(step, 0, start_block)
+            when_in(step, LEAD + 4, multiply_mid)
             return carry
 
-        lax.fori_loop(0, chunks + LEAD + 3, step_mid, 0)
+        lax.fori_loop(0, chunks + LEAD + 4, step_mid, 0)
 
         def finish(n, carry):
             along(own, 1, n, 0, inner).wait_send()
@@ -342,12 +350,12 @@
             multiply(n, choose)
 
         def step_end(step, carry):
+            when_in(step, LEAD, take_own)
             when_in(step, 0, start_block)
-            when_in(step, LEAD, take_own)
-            when_in(step, LEAD + 5, take_both)
+            when_in(step, LEAD + 7, take_both)
             return carry
 
-        lax.fori_loop(0, chunks + LEAD + 5, step_end, 0)
+        lax.fori_loop(0, chunks + LEAD + 7, step_end, 0)
 
         def finish(n, carry):
             along(own, 0, n, 0, next_in).wait_send()
@@ -360,6 +368,7 @@
         return carry
 
     lax.fori_loop(0, chunks, finish_all, 0)
+
     for pair in range(pairs):
         flush(pair).wait()
 
@@ -374,16 +383,17 @@
     bins, windows = F // owners, samples_here // WL
     chunks = (windows // GROUP) * (bins // PER_CHUNK)
     block = (chunks, PER_CHUNK, owners * 2 * GROUP, channels)
-    taps = jnp.pad(fir_taps[None, :], ((0, 0), (0, LEFT + WL + LEFT - TAPS)))
-    in_vmem = pl.BlockSpec(memory_space=pltpu.VMEM)
     in_place = pl.BlockSpec(memory_space=pl.ANY)
     result = (bins, ROUNDS, 2, channels, channels)
     return pl.pallas_call(
         functools.partial(exchange_kernel, owners, bins, windows, scale),
         out_shape=jax.ShapeDtypeStruct(result, jnp.bfloat16),
-        in_specs=[pl.BlockSpec(memory_space=pltpu.SMEM), in_place, in_vmem, in_vmem],
+        in_specs=[in_place] * 4,
         out_specs=in_place,
         scratch_shapes=[
+            pltpu.SMEM(plan.shape, jnp.int32),
+            pltpu.VMEM((1, TAPS), jnp.float32),
+            pltpu.VMEM((2 * F, WL), jnp.float32),
             pltpu.VMEM(records.shape, jnp.bfloat16),
             pltpu.VMEM((4 * F, LEFT + WL), jnp.bfloat16),
             pltpu.VMEM((channels, LEFT), jnp.bfloat16),
@@ -392,8 +402,9 @@
             pltpu.VMEM(block, jnp.bfloat16),
             pltpu.VMEM((3,) + block, jnp.bfloat16),
             pltpu.VMEM((2,) + block, jnp.bfloat16),
-            pltpu.VMEM((bins, ROUNDS, channels, 2 * channels), jnp.float32),
+            pltpu.VMEM(result, jnp.float32),
             pltpu.VMEM(result, jnp.bfloat16),
+            pltpu.SemaphoreType.DMA((3,)),
             pltpu.SemaphoreType.DMA((windows // GROUP,)),
             pltpu.SemaphoreType.DMA,
             pltpu.SemaphoreType.DMA,
@@ -407,7 +418,7 @@
             collective_id=0, has_side_effects=True, vmem_limit_bytes=48 * 1024 * 1024
         ),
         name="exchange",
-    )(plan, records, taps, jnp.asarray(dft_rows(owners)))
+    )(plan, records, fir_taps[None, :], jnp.asarray(dft_rows(owners)))
 
 
 def cross_kernel(scale, groups, rows, slots, own, first, second, out):

time: 141 us -> 140 us (level)
  no operation moved by 1% of the time
where the time goes in v4:
time: 140 us
  Pallas kernels  133 us (95%)
  other arithmetic  4.45 us (3%)
  local copies, waits for them, and re-layouts  2.24 us (2%)
    pallas_call x1, Pallas kernels, exchange(): pl.pallas_call(functools.partial(exchange_kernel, owners, bins, windows,...  133 us
    convert_element_type x1, other arithmetic, on_device(): return exchange(records, fir_taps, plan, scale).astype(jnp.float32)  4.45 us

profile of v4, /device:TPU:0, one launch (start us, length us, event | category | flops | bytes accessed | tf_op | source)
XLA Modules:
  0.0 139.9 jit_solution(647769602298809626)
XLA Ops:
  0.0 0.0 copy-start
  0.0 0.9 copy-done
  0.9 0.0 copy-start.1
  0.9 0.7 copy-done.1
  1.6 0.0 copy-start.2
  1.6 0.7 copy-done.2
  2.2 133.2 %exchange.1 = bf16[8,2,2,256,256]{4,3,2,1,0:T(8,128)(2,1)S(1)} custom-call(s32[2,4]{1,0:T(2,128)S(1)} %copy-done.1, bf16[256,10240]{1,0:T(8,128)(2,1)} %records.1, f32[1,64]{1,0:T(1,128)S(1)} %bitcast.1, f32[128,256]{1,0:T(8,128)S(1)} %copy-done), custom_call_target="tpu_custom_call" | custom-call | tf_op jit(solution)/shard_map/exchange/pallas_call | solution.py:388
  135.5 4.5 %convert_element_type.3 = f32[8,2,2,256,256]{4,3,2,1,0:T(8,128)} convert(bf16[8,2,2,256,256]{4,3,2,1,0:T(8,128)(2,1)S(1)} %exchange.1) | non-fusion elementwise | flops 2097152 | bytes 12582912 | tf_op jit(solution)/shard_map/convert_element_type | solution.py:482
Async XLA Ops:
  0.0 0.9 copy-start
  0.9 0.7 copy-start.1
  1.6 0.7 copy-start.2

commit v5 on v4

--- a/solution.py
+++ b/solution.py
@@ -16,7 +16,8 @@
 LEFT = 128
 GROUP = 8
 PER_CHUNK = 1
-LEAD = 4
+LEAD = 2
+SETTLE = LEAD + 12
 MESH = pl.DeviceIdType.MESH
 
 
@@ -278,6 +279,18 @@
         def _():
             body(n)
 
+    def sent(n):
+        pltpu.make_async_copy(own.at[n, :, others], own.at[n, :, others], a2a_send.at[n]).wait()
+
+    def run(steps, body, finish):
+        lax.fori_loop(0, steps, body, 0)
+
+        def rest(n, carry):
+            finish(n)
+            return carry
+
+        lax.fori_loop(steps - SETTLE, chunks, rest, 0)
+
     keys = [plan[index, 0] for index in range(ROUNDS)]
     has_1 = jnp.logical_or(keys[0] == 1, keys[1] == 1)
     has_3 = jnp.logical_or(keys[0] == 3, keys[1] == 3)
@@ -310,25 +323,24 @@
 
             multiply(n, choose)
 
-        def step_mid(step, carry):
-            when_in(step, LEAD, take_own)
-            when_in(step, LEAD + 1, take_outer)
-            when_in(step, LEAD + 2, take_inner)
-            when_in(step, LEAD + 4, take_far)
-            when_in(step, 0, start_block)
-            when_in(step, LEAD + 4, multiply_mid)
-            return carry
-
-        lax.fori_loop(0, chunks + LEAD + 4, step_mid, 0)
-
-        def finish(n, carry):
+        def finish(n):
+            sent(n)
             along(own, 1, n, 0, inner).wait_send()
             along(recv.at[0], 2, n, 1, inner).wait_send()
             along(stage.at[0], 0, n, 2, outer).wait_send()
             along(stage.at[1], 1, n, 3, outer).wait_send()
+
+        def step_mid(step, carry):
+            when_in(step, LEAD, take_own)
+            when_in(step, LEAD + 2, take_inner)
+            when_in(step, LEAD + 2, take_outer)
+            when_in(step, LEAD + 4, take_far)
+            when_in(step, 0, start_block)
+            when_in(step, LEAD + 4, multiply_mid)
+            when_in(step, SETTLE, finish)
             return carry
 
-        lax.fori_loop(0, chunks, finish, 0)
+        run(chunks + LEAD + 4, step_mid, finish)
 
     @pl.when(is_end)
     def _():
@@ -349,25 +361,19 @@
 
             multiply(n, choose)
 
+        def finish(n):
+            sent(n)
+            along(own, 0, n, 0, next_in).wait_send()
+
         def step_end(step, carry):
             when_in(step, LEAD, take_own)
             when_in(step, 0, start_block)
+            when_in(step, SETTLE, finish)
             when_in(step, LEAD + 7, take_both)
             return carry
 
-        lax.fori_loop(0, chunks + LEAD + 7, step_end, 0)
-
-        def finish(n, carry):
-            along(own, 0, n, 0, next_in).wait_send()
-            return carry
-
-        lax.fori_loop(0, chunks, finish, 0)
-
-    def finish_all(n, carry):
-        pltpu.make_async_copy(own.at[n, :, others], own.at[n, :, others], a2a_send.at[n]).wait()
-        return carry
-
-    lax.fori_loop(0, chunks, finish_all, 0)
+        run(chunks + LEAD + 7, step_end, finish)
+
 
     for pair in range(pairs):
         flush(pair).wait()

time: 140 us -> 139 us (level)
  no operation moved by 1% of the time
where the time goes in v5:
time: 139 us
  Pallas kernels  132 us (95%)
  other arithmetic  4.45 us (3%)
  local copies, waits for them, and re-layouts  2.24 us (2%)
    pallas_call x1, Pallas kernels, exchange(): pl.pallas_call(functools.partial(exchange_kernel, owners, bins, windows,...  132 us
    convert_element_type x1, other arithmetic, on_device(): return exchange(records, fir_taps, plan, scale).astype(jnp.float32)  4.45 us

profile of v5, /device:TPU:0, one launch (start us, length us, event | category | flops | bytes accessed | tf_op | source)
XLA Modules:
  0.0 138.9 jit_solution(9303503359204406377)
XLA Ops:
  0.0 0.0 copy-start
  0.0 0.9 copy-done
  0.9 0.0 copy-start.1
  0.9 0.7 copy-done.1
  1.6 0.0 copy-start.2
  1.6 0.7 copy-done.2
  2.2 132.2 %exchange.1 = bf16[8,2,2,256,256]{4,3,2,1,0:T(8,128)(2,1)S(1)} custom-call(s32[2,4]{1,0:T(2,128)S(1)} %copy-done.1, bf16[256,10240]{1,0:T(8,128)(2,1)} %records.1, f32[1,64]{1,0:T(1,128)S(1)} %bitcast.1, f32[128,256]{1,0:T(8,128)S(1)} %copy-done), custom_call_target="tpu_custom_call" | custom-call | tf_op jit(solution)/shard_map/exchange/pallas_call | solution.py:394
  134.4 4.5 %convert_element_type.3 = f32[8,2,2,256,256]{4,3,2,1,0:T(8,128)} convert(bf16[8,2,2,256,256]{4,3,2,1,0:T(8,128)(2,1)S(1)} %exchange.1) | non-fusion elementwise | flops 2097152 | bytes 12582912 | tf_op jit(solution)/shard_map/convert_element_type | solution.py:488
Async XLA Ops:
  0.0 0.9 copy-start
  0.9 0.7 copy-start.1
  1.6 0.7 copy-start.2

commit v6 on v5

--- a/solution.py
+++ b/solution.py
@@ -149,19 +149,6 @@
     table[:kept] = high
     table[kept:] = (combined - high.astype(jnp.float32)).astype(jnp.bfloat16)
 
-    pl.semaphore_wait(barrier, jnp.where(is_mid, owners + 1, owners))
-
-    def tail_copy():
-        return pltpu.make_async_remote_copy(
-            src_ref=records.at[:, pl.ds(windows * WL - LEFT, LEFT)], dst_ref=halo,
-            send_sem=halo_send, recv_sem=halo_recv,
-            device_id={"win": lax.rem(me + 1, owners)}, device_id_type=MESH,
-        )
-
-    @pl.when(me < owners - 1)
-    def _():
-        tail_copy().start()
-
     def whiten_window(place, segment):
         both = lax.dot_general(
             table[...], segment, (((1,), (1,)), ((), ())), preferred_element_type=jnp.float32
@@ -201,12 +188,26 @@
             start = pl.multiple_of(base + place * WL - LEFT, LEFT)
             whiten_window(place, rec[:, pl.ds(start, LEFT + WL)])
 
+    whiten_group(jnp.int32(0))
+    pl.semaphore_wait(barrier, jnp.where(is_mid, owners + 1, owners))
+
+    def tail_copy():
+        return pltpu.make_async_remote_copy(
+            src_ref=records.at[:, pl.ds(windows * WL - LEFT, LEFT)], dst_ref=halo,
+            send_sem=halo_send, recv_sem=halo_recv,
+            device_id={"win": lax.rem(me + 1, owners)}, device_id_type=MESH,
+        )
+
+    @pl.when(me < owners - 1)
+    def _():
+        tail_copy().start()
+
     mine = pl.ds(pl.multiple_of(me * unit, unit), unit)
 
     def start_block(n):
         pair = lax.rem(n, pairs)
 
-        @pl.when(pair == 0)
+        @pl.when(jnp.logical_and(pair == 0, n > 0))
         def _():
             whiten_group(n // pairs)
 
@@ -421,7 +422,7 @@
             pltpu.SemaphoreType.DMA((bins // PER_CHUNK,)),
         ],
         compiler_params=pltpu.CompilerParams(
-            collective_id=0, has_side_effects=True, vmem_limit_bytes=48 * 1024 * 1024
+            collective_id=0, has_side_effects=True, vmem_limit_bytes=63 * 1024 * 1024
         ),
         name="exchange",
     )(plan, records, fir_taps[None, :], jnp.asarray(dft_rows(owners)))

time: 139 us -> 140 us (level)
  local copies, waits for them, and re-layouts: 2.24 us -> 0 us
  other arithmetic: 4.45 us -> 6.64 us
  Pallas kernels: 132 us -> 134 us
    unnamed x6 -> x0, local copies, waits for them, and re-layouts: 2.24 us -> none
    convert_element_type x1, other arithmetic: 4.45 us -> 6.64 us  [on_device(): return exchange(records, fir_taps, plan, scale).astype(jnp.float32)]
    pallas_call x1, Pallas kernels: 132 us -> 134 us  [exchange(): pl.pallas_call(functools.partial(exchange_kernel, owners, bins, windows,...]
where the time goes in v6:
time: 140 us
  Pallas kernels  134 us (96%)
  other arithmetic  6.64 us (5%)
    pallas_call x1, Pallas kernels, exchange(): pl.pallas_call(functools.partial(exchange_kernel, owners, bins, windows,...  134 us
    convert_element_type x1, other arithmetic, on_device(): return exchange(records, fir_taps, plan, scale).astype(jnp.float32)  6.64 us

profile of v6, /device:TPU:0, one launch (start us, length us, event | category | flops | bytes accessed | tf_op | source)
XLA Modules:
  0.0 140.3 jit_solution(2031253645301887089)
XLA Ops:
  0.0 133.6 %exchange.1 = bf16[8,2,2,256,256]{4,3,2,1,0:T(8,128)(2,1)} custom-call(s32[2,4]{1,0:T(2,128)} %plan_at.1, bf16[256,10240]{1,0:T(8,128)(2,1)} %records.1, f32[1,64]{1,0:T(1,128)} %bitcast.1, f32[128,256]{1,0:T(8,128)} %constant.2.clone.dft_at), custom_call_target="tpu_custom_call" | custom-call | tf_op jit(solution)/shard_map/exchange/pallas_call | solution.py:395
  133.6 6.6 %convert_element_type.3 = f32[8,2,2,256,256]{4,3,2,1,0:T(8,128)} convert(bf16[8,2,2,256,256]{4,3,2,1,0:T(8,128)(2,1)} %exchange.1) | non-fusion elementwise | flops 2097152 | bytes 12582912 | tf_op jit(solution)/shard_map/convert_element_type | solution.py:489

commit v7 on v6

--- a/solution.py
+++ b/solution.py
@@ -92,9 +92,9 @@
     return np.where(part == 0, np.cos(phases), -np.sin(phases)).astype(np.float32)
 
 
-def exchange_kernel(owners, bins, windows, scale, plan_at, records, taps_at, dft_at, out,
-                    plan, taps, dft, rec, table, halo, spectra, x, own, recv, stage, acc, result,
-                    small_sem, rec_sem, halo_send, halo_recv, a2a_send, a2a_recv, z_send, z_recv, out_sem):
+def exchange_kernel(owners, bins, windows, scale, plan_at, records, taps, dft, out,
+                    plan, rec, table, halo, spectra, x, own, recv, stage, acc, result,
+                    plan_sem, rec_sem, halo_send, halo_recv, a2a_send, a2a_recv, z_send, z_recv, out_sem):
     chan = lax.axis_index("chan")
     me = lax.axis_index("win")
     is_mid = jnp.logical_and(chan >= 1, chan <= 2)
@@ -114,12 +114,8 @@
         columns = pl.ds(pl.multiple_of(g * span, span), span)
         return pltpu.make_async_copy(records.at[:, columns], rec.at[:, columns], rec_sem.at[g])
 
-    small = [
-        pltpu.make_async_copy(source, target, small_sem.at[place])
-        for place, (source, target) in enumerate(((taps_at, taps), (dft_at, dft), (plan_at, plan)))
-    ]
-    for copy in small:
-        copy.start()
+    plan_copy = pltpu.make_async_copy(plan_at, plan, plan_sem)
+    plan_copy.start()
     for g in range(groups):
         load(g).start()
 
@@ -136,8 +132,6 @@
     def _():
         pl.semaphore_signal(barrier, inc=1, device_id={"chan": next_in}, device_id_type=MESH)
 
-    for copy in small:
-        copy.wait()
     row = jnp.concatenate([taps[...], jnp.zeros((1, LEFT + WL + LEFT - TAPS), jnp.float32)], axis=1)
     spread = jnp.broadcast_to(row, (LEFT + WL, LEFT + WL + LEFT))
     shifted_taps = pltpu.roll(spread, 0, 1, stride=1, stride_axis=0)[:, LEFT : LEFT + WL]
@@ -292,6 +286,7 @@
 
         lax.fori_loop(steps - SETTLE, chunks, rest, 0)
 
+    plan_copy.wait()
     keys = [plan[index, 0] for index in range(ROUNDS)]
     has_1 = jnp.logical_or(keys[0] == 1, keys[1] == 1)
     has_3 = jnp.logical_or(keys[0] == 3, keys[1] == 3)
@@ -391,16 +386,15 @@
     chunks = (windows // GROUP) * (bins // PER_CHUNK)
     block = (chunks, PER_CHUNK, owners * 2 * GROUP, channels)
     in_place = pl.BlockSpec(memory_space=pl.ANY)
+    in_vmem = pl.BlockSpec(memory_space=pltpu.VMEM)
     result = (bins, ROUNDS, 2, channels, channels)
     return pl.pallas_call(
         functools.partial(exchange_kernel, owners, bins, windows, scale),
         out_shape=jax.ShapeDtypeStruct(result, jnp.bfloat16),
-        in_specs=[in_place] * 4,
+        in_specs=[in_place, in_place, in_vmem, in_vmem],
         out_specs=in_place,
         scratch_shapes=[
             pltpu.SMEM(plan.shape, jnp.int32),
-            pltpu.VMEM((1, TAPS), jnp.float32),
-            pltpu.VMEM((2 * F, WL), jnp.float32),
             pltpu.VMEM(records.shape, jnp.bfloat16),
             pltpu.VMEM((4 * F, LEFT + WL), jnp.bfloat16),
             pltpu.VMEM((channels, LEFT), jnp.bfloat16),
@@ -411,7 +405,7 @@
             pltpu.VMEM((2,) + block, jnp.bfloat16),
             pltpu.VMEM(result, jnp.float32),
             pltpu.VMEM(result, jnp.bfloat16),
-            pltpu.SemaphoreType.DMA((3,)),
+            pltpu.SemaphoreType.DMA,
             pltpu.SemaphoreType.DMA((windows // GROUP,)),
             pltpu.SemaphoreType.DMA,
             pltpu.SemaphoreType.DMA,
@@ -422,10 +416,36 @@
             pltpu.SemaphoreType.DMA((bins // PER_CHUNK,)),
         ],
         compiler_params=pltpu.CompilerParams(
-            collective_id=0, has_side_effects=True, vmem_limit_bytes=63 * 1024 * 1024
+            collective_id=0, has_side_effects=True, vmem_limit_bytes=48 * 1024 * 1024
         ),
         name="exchange",
     )(plan, records, fir_taps[None, :], jnp.asarray(dft_rows(owners)))
+
+
+def widen_kernel(narrow, out, wide, sems):
+    def copy(place):
+        return pltpu.make_async_copy(wide.at[place], out.at[place], sems.at[place])
+
+    for place in range(narrow.shape[0]):
+        wide[place] = narrow[place].astype(jnp.float32)
+        copy(place).start()
+    for place in range(narrow.shape[0]):
+        copy(place).wait()
+
+
+def widen(narrow):
+    return pl.pallas_call(
+        widen_kernel,
+        out_shape=jax.ShapeDtypeStruct(narrow.shape, jnp.float32),
+        in_specs=[pl.BlockSpec(memory_space=pltpu.VMEM)],
+        out_specs=pl.BlockSpec(memory_space=pl.ANY),
+        scratch_shapes=[
+            pltpu.VMEM(narrow.shape, jnp.float32),
+            pltpu.SemaphoreType.DMA((narrow.shape[0],)),
+        ],
+        compiler_params=pltpu.CompilerParams(vmem_limit_bytes=24 * 1024 * 1024),
+        name="widen",
+    )(narrow)
 
 
 def cross_kernel(scale, groups, rows, slots, own, first, second, out):
@@ -486,7 +506,7 @@
     scale = 1.0 / math.sqrt(window_count * owners)
     keys = jnp.bitwise_xor(plan[:, chan], chan)
     if lax.axis_size("chan") == 4:
-        return exchange(records, fir_taps, plan, scale).astype(jnp.float32)
+        return widen(exchange(records, fir_taps, plan, scale))
     whitened = whiten(records, fir_taps)
     gathered = gather_images(
         whitened.reshape(owners, F // owners, 2 * window_count, channels)

time: 140 us -> 138 us (0.986)
  other arithmetic: 6.64 us -> 0 us
  local copies, waits for them, and re-layouts: 0 us -> 2.24 us
    convert_element_type x1 -> x0, other arithmetic: 6.64 us -> none  [on_device(): return exchange(records, fir_taps, plan, scale).astype(jnp.float32)]
    pallas_call x0 -> x1, Pallas kernels: none -> 3.44 us  [widen(): pl.pallas_call(widen_kernel, out_shape=jax.ShapeDtypeStruct(narrow.shape,...]
    unnamed x0 -> x6, local copies, waits for them, and re-layouts: none -> 2.24 us
    pallas_call x1, Pallas kernels: 134 us -> 132 us  [exchange(): pl.pallas_call(functools.partial(exchange_kernel, owners, bins, windows,...]
where the time goes in v7:
time: 138 us
  Pallas kernels  135 us (98%)
  local copies, waits for them, and re-layouts  2.24 us (2%)
    pallas_call x1, Pallas kernels, exchange(): pl.pallas_call(functools.partial(exchange_kernel, owners, bins, windows,...  132 us
    pallas_call x1, Pallas kernels, widen(): pl.pallas_call(widen_kernel, out_shape=jax.ShapeDtypeStruct(narrow.shape,...  3.44 us

profile of v7, /device:TPU:0, one launch (start us, length us, event | category | flops | bytes accessed | tf_op | source)
XLA Modules:
  0.0 137.7 jit_solution(4132544017942346912)
XLA Ops:
  0.0 0.0 copy-start
  0.0 0.9 copy-done
  0.9 0.0 copy-start.1
  0.9 0.7 copy-done.1
  1.6 0.0 copy-start.2
  1.6 0.7 copy-done.2
  2.2 132.0 %exchange.1.narrow = bf16[8,2,2,256,256]{4,3,2,1,0:T(8,128)(2,1)S(1)} custom-call(s32[2,4]{1,0:T(2,128)S(1)} %copy-done.1, bf16[256,10240]{1,0:T(8,128)(2,1)} %records.1, f32[1,64]{1,0:T(1,128)S(1)} %bitcast.1, f32[128,256]{1,0:T(8,128)S(1)} %copy-done), custom_call_target="tpu_custom_call" | custom-call | tf_op jit(solution)/shard_map/exchange/pallas_call | solution.py:391
  134.2 3.4 %widen.1 = f32[8,2,2,256,256]{4,3,2,1,0:T(8,128)} custom-call(bf16[8,2,2,256,256]{4,3,2,1,0:T(8,128)(2,1)S(1)} %exchange.1.narrow), custom_call_target="tpu_custom_call" | custom-call | tf_op jit(solution)/shard_map/widen/pallas_call | solution.py:437
Async XLA Ops:
  0.0 0.9 copy-start
  0.9 0.7 copy-start.1
  1.6 0.7 copy-start.2

commit v8 on v7

--- a/solution.py
+++ b/solution.py
@@ -103,7 +103,7 @@
     outer = 3 * (chan - 1)
     next_in = 1 + chan // 3
     kept = 2 * F
-    lanes = spectra.shape[0]
+    lanes = spectra.shape[0] // 2
     groups = windows // GROUP
     pairs = bins // PER_CHUNK
     chunks = groups * pairs
@@ -143,7 +143,7 @@
     table[:kept] = high
     table[kept:] = (combined - high.astype(jnp.float32)).astype(jnp.bfloat16)
 
-    def whiten_window(place, segment):
+    def whiten_window(turn, place, segment):
         both = lax.dot_general(
             table[...], segment, (((1,), (1,)), ((), ())), preferred_element_type=jnp.float32
         )
@@ -151,38 +151,42 @@
         power = jnp.mean(stacked * stacked, axis=0, keepdims=True) + 1e-06
         whitened = stacked * (1.0 / jnp.sqrt(power))
         for lane in range(lanes):
-            spectra[lane, pl.ds(place * kept, kept)] = whitened[:, lane * 128 : lane * 128 + 128]
-
-    def whiten_group(turn):
+            rows = pl.ds(pl.multiple_of(place * kept, kept), kept)
+            spectra[lax.rem(turn, 2) * lanes + lane, rows] = whitened[
+                :, lane * 128 : lane * 128 + 128
+            ]
+
+    def whiten_ahead(step):
+        turn, place = step // GROUP, lax.rem(step, GROUP)
         g = lax.rem(turn + 1, groups)
-        base = g * span
-
-        @pl.when(turn == 0)
-        def _():
-            load(0).wait()
-
-        @pl.when(g > 0)
+        w = g * GROUP + place
+
+        @pl.when(jnp.logical_and(place == 0, g > 0))
         def _():
             load(g).wait()
-            whiten_window(0, rec[:, pl.ds(pl.multiple_of(base - LEFT, LEFT), LEFT + WL)])
-
-        @pl.when(jnp.logical_and(g == 0, me == 0))
+
+        @pl.when(w > 0)
+        def _():
+            start = pl.multiple_of(w * WL - LEFT, LEFT)
+            whiten_window(turn, place, rec[:, pl.ds(start, LEFT + WL)])
+
+        @pl.when(jnp.logical_and(w == 0, me == 0))
         def _():
             halo[...] = jnp.zeros_like(halo)
 
-        @pl.when(jnp.logical_and(g == 0, me > 0))
+        @pl.when(jnp.logical_and(w == 0, me > 0))
         def _():
             pltpu.make_async_copy(halo, halo, halo_recv).wait()
 
-        @pl.when(g == 0)
-        def _():
-            whiten_window(0, jnp.concatenate([halo[...], rec[:, :WL]], axis=1))
-
-        for place in range(1, GROUP):
-            start = pl.multiple_of(base + place * WL - LEFT, LEFT)
-            whiten_window(place, rec[:, pl.ds(start, LEFT + WL)])
-
-    whiten_group(jnp.int32(0))
+        @pl.when(w == 0)
+        def _():
+            whiten_window(turn, place, jnp.concatenate([halo[...], rec[:, :WL]], axis=1))
+
+    load(0).wait()
+    load(1).wait()
+    for place in range(GROUP):
+        start = span + place * WL - LEFT
+        whiten_window(0, place, rec[:, start : start + LEFT + WL])
     pl.semaphore_wait(barrier, jnp.where(is_mid, owners + 1, owners))
 
     def tail_copy():
@@ -201,16 +205,13 @@
     def start_block(n):
         pair = lax.rem(n, pairs)
 
-        @pl.when(jnp.logical_and(pair == 0, n > 0))
-        def _():
-            whiten_group(n // pairs)
-
+        half = lax.rem(n // pairs, 2) * lanes
         for b in range(PER_CHUNK):
             for owner in range(owners):
                 first = ((pair * PER_CHUNK + b) * owners + owner) * 2
                 for lane in range(lanes):
-                    real = spectra[lane, pl.ds(first, GROUP, stride=kept)]
-                    imag = spectra[lane, pl.ds(first + 1, GROUP, stride=kept)]
+                    real = spectra[half + lane, pl.ds(first, GROUP, stride=kept)]
+                    imag = spectra[half + lane, pl.ds(first + 1, GROUP, stride=kept)]
                     x[n, owner, b, :, lane * 128 : lane * 128 + 128] = jnp.concatenate(
                         [real, imag], axis=0
                     ).astype(jnp.bfloat16)
@@ -274,6 +275,11 @@
         def _():
             body(n)
 
+    def when_ahead(step):
+        @pl.when(step < chunks - pairs)
+        def _():
+            whiten_ahead(step + GROUP)
+
     def sent(n):
         pltpu.make_async_copy(own.at[n, :, others], own.at[n, :, others], a2a_send.at[n]).wait()
 
@@ -334,6 +340,7 @@
             when_in(step, 0, start_block)
             when_in(step, LEAD + 4, multiply_mid)
             when_in(step, SETTLE, finish)
+            when_ahead(step)
             return carry
 
         run(chunks + LEAD + 4, step_mid, finish)
@@ -366,6 +373,7 @@
             when_in(step, 0, start_block)
             when_in(step, SETTLE, finish)
             when_in(step, LEAD + 7, take_both)
+            when_ahead(step)
             return carry
 
         run(chunks + LEAD + 7, step_end, finish)
@@ -398,7 +406,7 @@
             pltpu.VMEM(records.shape, jnp.bfloat16),
             pltpu.VMEM((4 * F, LEFT + WL), jnp.bfloat16),
             pltpu.VMEM((channels, LEFT), jnp.bfloat16),
-            pltpu.VMEM((channels // 128, GROUP * 2 * F, 128), jnp.float32),
+            pltpu.VMEM((channels // 128 * 2, GROUP * 2 * F, 128), jnp.float32),
             pltpu.VMEM((chunks, owners, PER_CHUNK, 2 * GROUP, channels), jnp.bfloat16),
             pltpu.VMEM(block, jnp.bfloat16),
             pltpu.VMEM((3,) + block, jnp.bfloat16),
@@ -505,7 +513,7 @@
     chan = lax.axis_index("chan")
     scale = 1.0 / math.sqrt(window_count * owners)
     keys = jnp.bitwise_xor(plan[:, chan], chan)
-    if lax.axis_size("chan") == 4:
+    if lax.axis_size("chan") == 4 and F // owners == GROUP * PER_CHUNK:
         return widen(exchange(records, fir_taps, plan, scale))
     whitened = whiten(records, fir_taps)
     gathered = gather_images(

time: 138 us -> 138 us (level)
  no operation moved by 1% of the time
where the time goes in v8:
time: 138 us; the launch traced here: 137 us
  Pallas kernels  135 us (98%)
  local copies, waits for them, and re-layouts  2.24 us (2%)
    pallas_call x1, Pallas kernels, exchange(): pl.pallas_call(functools.partial(exchange_kernel, owners, bins, windows,...  132 us
    pallas_call x1, Pallas kernels, widen(): pl.pallas_call(widen_kernel, out_shape=jax.ShapeDtypeStruct(narrow.shape,...  3.44 us

profile of v8, /device:TPU:0, one launch (start us, length us, event | category | flops | bytes accessed | tf_op | source)
XLA Modules:
  0.0 137.4 jit_solution(2823257221662138559)
XLA Ops:
  0.0 0.0 copy-start
  0.0 0.9 copy-done
  0.9 0.0 copy-start.1
  0.9 0.7 copy-done.1
  1.6 0.0 copy-start.2
  1.6 0.7 copy-done.2
  2.2 131.7 %exchange.1.narrow = bf16[8,2,2,256,256]{4,3,2,1,0:T(8,128)(2,1)S(1)} custom-call(s32[2,4]{1,0:T(2,128)S(1)} %copy-done.1, bf16[256,10240]{1,0:T(8,128)(2,1)} %records.1, f32[1,64]{1,0:T(1,128)S(1)} %bitcast.1, f32[128,256]{1,0:T(8,128)S(1)} %copy-done), custom_call_target="tpu_custom_call" | custom-call | tf_op jit(solution)/shard_map/exchange/pallas_call | solution.py:399
  134.0 3.4 %widen.1 = f32[8,2,2,256,256]{4,3,2,1,0:T(8,128)} custom-call(bf16[8,2,2,256,256]{4,3,2,1,0:T(8,128)(2,1)S(1)} %exchange.1.narrow), custom_call_target="tpu_custom_call" | custom-call | tf_op jit(solution)/shard_map/widen/pallas_call | solution.py:445
Async XLA Ops:
  0.0 0.9 copy-start
  0.9 0.7 copy-start.1
  1.6 0.7 copy-start.2

commit v9 on v8

--- a/solution.py
+++ b/solution.py
@@ -334,16 +334,16 @@
 
         def step_mid(step, carry):
             when_in(step, LEAD, take_own)
-            when_in(step, LEAD + 2, take_inner)
+            when_in(step, LEAD + 1, take_inner)
             when_in(step, LEAD + 2, take_outer)
-            when_in(step, LEAD + 4, take_far)
+            when_in(step, LEAD + 3, take_far)
             when_in(step, 0, start_block)
-            when_in(step, LEAD + 4, multiply_mid)
+            when_in(step, LEAD + 3, multiply_mid)
             when_in(step, SETTLE, finish)
             when_ahead(step)
             return carry
 
-        run(chunks + LEAD + 4, step_mid, finish)
+        run(chunks + LEAD + 3, step_mid, finish)
 
     @pl.when(is_end)
     def _():

time: 138 us -> 139 us (level)
  Pallas kernels: 135 us -> 137 us
    pallas_call x1, Pallas kernels: 132 us -> 133 us  [exchange(): pl.pallas_call(functools.partial(exchange_kernel, owners, bins, windows,...]
where the time goes in v9:
time: 139 us
  Pallas kernels  137 us (99%)
  local copies, waits for them, and re-layouts  2.24 us (2%)
    pallas_call x1, Pallas kernels, exchange(): pl.pallas_call(functools.partial(exchange_kernel, owners, bins, windows,...  133 us
    pallas_call x1, Pallas kernels, widen(): pl.pallas_call(widen_kernel, out_shape=jax.ShapeDtypeStruct(narrow.shape,...  3.44 us

profile of v9, /device:TPU:0, one launch (start us, length us, event | category | flops | bytes accessed | tf_op | source)
XLA Modules:
  0.0 138.8 jit_solution(9082985985936680753)
XLA Ops:
  0.0 0.0 copy-start
  0.0 0.9 copy-done
  0.9 0.0 copy-start.1
  0.9 0.7 copy-done.1
  1.6 0.0 copy-start.2
  1.6 0.7 copy-done.2
  2.2 133.2 %exchange.1.narrow = bf16[8,2,2,256,256]{4,3,2,1,0:T(8,128)(2,1)S(1)} custom-call(s32[2,4]{1,0:T(2,128)S(1)} %copy-done.1, bf16[256,10240]{1,0:T(8,128)(2,1)} %records.1, f32[1,64]{1,0:T(1,128)S(1)} %bitcast.1, f32[128,256]{1,0:T(8,128)S(1)} %copy-done), custom_call_target="tpu_custom_call" | custom-call | tf_op jit(solution)/shard_map/exchange/pallas_call | solution.py:399
  135.4 3.4 %widen.1 = f32[8,2,2,256,256]{4,3,2,1,0:T(8,128)} custom-call(bf16[8,2,2,256,256]{4,3,2,1,0:T(8,128)(2,1)S(1)} %exchange.1.narrow), custom_call_target="tpu_custom_call" | custom-call | tf_op jit(solution)/shard_map/widen/pallas_call | solution.py:445
Async XLA Ops:
  0.0 0.9 copy-start
  0.9 0.7 copy-start.1
  1.6 0.7 copy-start.2
